TPU v7x, 32 devices: a whole 2x2x4 slice. The times are simulated.
32 devices in a mesh: dp: 8 (over z, y), seq: 4 (over x, core).
Axes of the slice: x: 2, y: 2, z: 4, core: 2. Of those that a mesh axis runs over, the one named last changes fastest.
Arguments:
- inputs: bfloat16 [8192, 1024], P(('dp', 'seq')), may hold values from -6 to 6
- doc_starts: int32 [8, 4], P('dp'), may hold values from 0 to 1023, as said below
- cotangent: bfloat16 [8192, 1024], P(('dp', 'seq')), may hold values from -6 to 6
- attn_gain: bfloat16 [1024], P(('dp', 'seq')), may hold values from 0.5 to 1.5
- w_query: bfloat16 [1024, 1024], P(('dp', 'seq')), may hold values from -0.1875 to 0.1875
- key_projection_weight: bfloat16 [1024, 512], P(('dp', 'seq')), may hold values from -0.1875 to 0.1875
- value_projection_weight: bfloat16 [1024, 512], P(('dp', 'seq')), may hold values from -0.1875 to 0.1875
- q_gain: bfloat16 [64], replicated, may hold values from 0.099609375 to 1.8984375
- k_gain: bfloat16 [64], replicated, may hold values from 0.099609375 to 1.8984375
- w_out: bfloat16 [1024, 1024], P(('dp', 'seq')), may hold values from -1 to 1
- ffn_gain: bfloat16 [1024], P(('dp', 'seq')), may hold values from 0.5 to 1.5
- w_gate: bfloat16 [1024, 4608], P(('dp', 'seq')), may hold values from -0.1875 to 0.1875
- w_up: bfloat16 [1024, 4608], P(('dp', 'seq')), may hold values from -0.1875 to 0.1875
- w_down: bfloat16 [4608, 1024], P(('dp', 'seq')), may hold values from -0.09375 to 0.09375
Outputs:
- output: bfloat16 [8192, 1024], P(('dp', 'seq'))
- input_grad: float32 [8192, 1024], P(('dp', 'seq'))
- attn_gain_grad: float32 [1024], P(('dp', 'seq'))
- query_grad: float32 [1024, 1024], P(('dp', 'seq'))
- key_grad: float32 [1024, 512], P(('dp', 'seq'))
- value_grad: float32 [1024, 512], P(('dp', 'seq'))
- q_gain_grad: float32 [64], replicated
- k_gain_grad: float32 [64], replicated
- out_grad: float32 [1024, 1024], P(('dp', 'seq'))
- ffn_gain_grad: float32 [1024], P(('dp', 'seq'))
- gate_grad: float32 [1024, 4608], P(('dp', 'seq'))
- up_grad: float32 [1024, 4608], P(('dp', 'seq'))
- down_grad: float32 [4608, 1024], P(('dp', 'seq'))
Inputs may be any that keep to these rules, and one draw needn't show every extreme that they name: `doc_starts`: each row holds 4 document starts, strictly increasing, the first 0; the second document starts within the first 256 positions of the row and ends within its last 256 positions.
All inputs are finite; a program needn't handle non-finite values.
Results may differ from a plain program's by a relative error of at most 0.015.
Values may be sent and summed in bfloat16 or wider, within the bound.
A program may use at most 320 MiB of HBM per device.

v0:
```python
import jax
import jax.numpy as jnp
from jax import lax
from jax.sharding import PartitionSpec as P

QUERY_HEADS = 16
KEY_VALUE_HEADS = 8
HEAD_SIZE = 64
FF = 4608


EPS = 1e-05
THETA = 1000000.0
MASKED = -1e30
CONTRACT_ROWS = (((0,), (0,)), ((), ()))
CONTRACT_COLS = (((1,), (1,)), ((), ()))


def rms_norm(values, gain_vec):
    return values * lax.rsqrt(jnp.mean(values * values, axis=-1, keepdims=True) + EPS) * gain_vec


def rotate_half(values):
    half_len = values.shape[-1] // 2
    return jnp.concatenate([-values[..., half_len:], values[..., :half_len]], axis=-1)


def unrotate_half(values):
    half_len = values.shape[-1] // 2
    return jnp.concatenate([values[..., half_len:], -values[..., :half_len]], axis=-1)


def row_layout(row_starts, places):
    inside = places[:, None] >= row_starts[None, :]
    doc_ids = jnp.sum(inside.astype(jnp.int32), axis=1) - 1
    begins = jnp.max(jnp.where(inside, row_starts[None, :], 0), axis=1)
    offsets = (places - begins).astype(jnp.float32)
    freq_steps = jnp.arange(HEAD_SIZE // 2, dtype=jnp.float32) * (2.0 / HEAD_SIZE)
    frequency = THETA ** (-freq_steps)
    angles = offsets[:, None] * frequency[None, :]
    angles = jnp.concatenate([angles, angles], axis=-1)
    return (doc_ids, jnp.cos(angles), jnp.sin(angles))


def norm_back(upstream, values, gain_vec):
    inverse = lax.rsqrt(jnp.mean(values * values, axis=-1, keepdims=True) + EPS)
    unit_vec = values * inverse
    gain_part = jnp.sum(upstream * unit_vec, axis=tuple(range(values.ndim - 1)))
    scaled = upstream * gain_vec
    return (
        inverse * (scaled - unit_vec * jnp.mean(scaled * unit_vec, axis=-1, keepdims=True)),
        gain_part,
    )


def head_forward_pass(linear, gain_vec, cosine_table, sine_table, heads):
    local_rows = linear.shape[0]
    shaped = rms_norm(linear.reshape(local_rows, heads, HEAD_SIZE), gain_vec)
    turned = shaped * cosine_table + rotate_half(shaped) * sine_table
    return turned.astype(jnp.bfloat16).reshape(local_rows, heads * HEAD_SIZE)


def head_backward_pass(grad_in, linear, gain_vec, cosine_table, sine_table, heads):
    local_rows = linear.shape[0]
    shaped = linear.reshape(local_rows, heads, HEAD_SIZE)
    upstream = grad_in.astype(jnp.float32).reshape(local_rows, heads, HEAD_SIZE)
    d_normed = upstream * cosine_table + unrotate_half(upstream * sine_table)
    d_linear, gain_part = norm_back(d_normed, shaped, gain_vec)
    return (d_linear.reshape(local_rows, heads * HEAD_SIZE).astype(jnp.bfloat16), gain_part)


def block_scores(q_block, keys_all, block_places, block_docs, places, doc_ids):
    score_scale = HEAD_SIZE ** (-0.5)
    scores = (
        jnp.einsum("qkgd,skd->kgqs", q_block, keys_all, preferred_element_type=jnp.float32)
        * score_scale
    )
    allowed = (places[None, :] <= block_places[:, None]) & (doc_ids[None, :] == block_docs[:, None])
    return jnp.where(allowed[None, None], scores, MASKED)


def attend_forward(query_rows, keys_in, values_in, places, doc_ids):
    total_length = query_rows.shape[0]
    kv_heads = keys_in.shape[1] // HEAD_SIZE
    query_group = QUERY_HEADS // KEY_VALUE_HEADS
    block_length = min(512, total_length)
    number_of_blocks = total_length // block_length
    keys_all = keys_in.reshape(total_length, kv_heads, HEAD_SIZE)
    values_all = values_in.reshape(total_length, kv_heads, HEAD_SIZE)
    grouped_queries = query_rows.reshape(
        number_of_blocks, block_length, kv_heads, query_group, HEAD_SIZE
    )

    def one_block(pieces):
        q_block, block_places, block_docs = pieces
        scores = block_scores(q_block, keys_all, block_places, block_docs, places, doc_ids)
        row_max = jnp.max(scores, axis=-1, keepdims=True)
        weights = jnp.exp(scores - row_max)
        sum_total = jnp.sum(weights, axis=-1, keepdims=True)
        soft_max = (weights / sum_total).astype(jnp.bfloat16)
        mixture = jnp.einsum(
            "kgqs,skd->qkgd", soft_max, values_all, preferred_element_type=jnp.float32
        )
        return (mixture.astype(jnp.bfloat16), row_max[..., 0] + jnp.log(sum_total[..., 0]))

    mixture, log_total = lax.map(
        one_block,
        (
            grouped_queries,
            places.reshape(number_of_blocks, block_length),
            doc_ids.reshape(number_of_blocks, block_length),
        ),
    )
    return (mixture.reshape(total_length, kv_heads * query_group * HEAD_SIZE), log_total)


def attend_back(query_rows, keys_in, values_in, grad_out, log_total, places, doc_ids):
    total_length = query_rows.shape[0]
    kv_heads = keys_in.shape[1] // HEAD_SIZE
    query_group = QUERY_HEADS // KEY_VALUE_HEADS
    block_length = min(512, total_length)
    number_of_blocks = total_length // block_length
    score_scale = HEAD_SIZE ** (-0.5)
    keys_all = keys_in.reshape(total_length, kv_heads, HEAD_SIZE)
    values_all = values_in.reshape(total_length, kv_heads, HEAD_SIZE)
    grouped_queries = query_rows.reshape(
        number_of_blocks, block_length, kv_heads, query_group, HEAD_SIZE
    )
    grads_all = grad_out.reshape(number_of_blocks, block_length, kv_heads, query_group, HEAD_SIZE)

    def one_block(carried, pieces):
        key_total, value_total = carried
        q_block, g_block, block_log, block_places, block_docs = pieces
        scores = block_scores(q_block, keys_all, block_places, block_docs, places, doc_ids)
        chances = jnp.exp(scores - block_log[..., None])
        d_chances = jnp.einsum(
            "qkgd,skd->kgqs", g_block, values_all, preferred_element_type=jnp.float32
        )
        row_dots = jnp.sum(d_chances * chances, axis=-1, keepdims=True)
        d_scores = (chances * (d_chances - row_dots)).astype(jnp.bfloat16)
        d_query = (
            jnp.einsum("kgqs,skd->qkgd", d_scores, keys_all, preferred_element_type=jnp.float32)
            * score_scale
        )
        key_total = (
            key_total
            + jnp.einsum("kgqs,qkgd->skd", d_scores, q_block, preferred_element_type=jnp.float32)
            * score_scale
        )
        value_total = value_total + jnp.einsum(
            "kgqs,qkgd->skd",
            chances.astype(jnp.bfloat16),
            g_block,
            preferred_element_type=jnp.float32,
        )
        return ((key_total, value_total), d_query)

    zero_kv = jnp.zeros((total_length, kv_heads, HEAD_SIZE), jnp.float32)
    inputs_scan = (
        grouped_queries,
        grads_all,
        log_total,
        places.reshape(number_of_blocks, block_length),
        doc_ids.reshape(number_of_blocks, block_length),
    )
    (key_total, value_total), d_query = lax.scan(one_block, (zero_kv, zero_kv), inputs_scan)
    return (
        d_query.reshape(total_length, kv_heads * query_group * HEAD_SIZE).astype(jnp.bfloat16),
        key_total.reshape(total_length, kv_heads * HEAD_SIZE).astype(jnp.bfloat16),
        value_total.reshape(total_length, kv_heads * HEAD_SIZE).astype(jnp.bfloat16),
    )


def on_device(
    inputs,
    doc_starts,
    cotangent,
    attn_gain,
    w_query,
    key_projection_weight,
    value_projection_weight,
    q_gain,
    k_gain,
    w_out,
    ffn_gain,
    w_gate,
    w_up,
    w_down,
):
    local_rows = inputs.shape[0]
    seq_parts = lax.axis_size("seq")
    total_length = local_rows * seq_parts
    row_starts = doc_starts[0]
    local_places = lax.axis_index("seq") * local_rows + jnp.arange(local_rows, dtype=jnp.int32)
    unused_docs, cosine_table, sine_table = row_layout(row_starts, local_places)
    cosine_table = cosine_table[:, None, :]
    sine_table = sine_table[:, None, :]
    all_places = jnp.arange(total_length, dtype=jnp.int32)
    all_docs = jnp.sum((all_places[:, None] >= row_starts[None, :]).astype(jnp.int32), axis=1) - 1
    q_scale = q_gain.astype(jnp.float32)
    key_norm_scale = k_gain.astype(jnp.float32)
    attn_scale, query_full, key_full, value_full, out_full = (
        lax.all_gather(attn_gain, ("dp", "seq"), axis=0, tiled=True),
        lax.all_gather(w_query, ("dp", "seq"), axis=0, tiled=True),
        lax.all_gather(key_projection_weight, ("dp", "seq"), axis=0, tiled=True),
        lax.all_gather(value_projection_weight, ("dp", "seq"), axis=0, tiled=True),
        lax.all_gather(w_out, ("dp", "seq"), axis=0, tiled=True),
    )
    source = inputs.astype(jnp.float32)
    normalized_input = rms_norm(source, attn_scale.astype(jnp.float32)).astype(jnp.bfloat16)
    q_linear = jnp.dot(normalized_input, query_full, preferred_element_type=jnp.float32)
    key_linear_output = jnp.dot(normalized_input, key_full, preferred_element_type=jnp.float32)
    q_sent = head_forward_pass(q_linear, q_scale, cosine_table, sine_table, QUERY_HEADS)
    key_sent_rows = head_forward_pass(
        key_linear_output, key_norm_scale, cosine_table, sine_table, KEY_VALUE_HEADS
    )
    v_sent = jnp.dot(normalized_input, value_full, preferred_element_type=jnp.float32).astype(
        jnp.bfloat16
    )
    q_heads, k_heads, v_heads = (
        lax.all_to_all(q_sent, "seq", split_axis=1, concat_axis=0, tiled=True),
        lax.all_to_all(key_sent_rows, "seq", split_axis=1, concat_axis=0, tiled=True),
        lax.all_to_all(v_sent, "seq", split_axis=1, concat_axis=0, tiled=True),
    )
    mixture, log_total = attend_forward(q_heads, k_heads, v_heads, all_places, all_docs)
    attended = lax.all_to_all(mixture, "seq", split_axis=0, concat_axis=1, tiled=True)
    middle = source + jnp.dot(attended, out_full, preferred_element_type=jnp.float32)
    ffn_scale, gate_full, up_full, down_full = (
        lax.all_gather(ffn_gain, ("dp", "seq"), axis=0, tiled=True),
        lax.all_gather(w_gate, ("dp", "seq"), axis=0, tiled=True),
        lax.all_gather(w_up, ("dp", "seq"), axis=0, tiled=True),
        lax.all_gather(w_down, ("dp", "seq"), axis=0, tiled=True),
    )
    normed_mid = rms_norm(middle, ffn_scale.astype(jnp.float32)).astype(jnp.bfloat16)
    gate_lin = jnp.dot(normed_mid, gate_full, preferred_element_type=jnp.float32)
    upward = jnp.dot(normed_mid, up_full, preferred_element_type=jnp.float32)
    sigmoid_gate = jax.nn.sigmoid(gate_lin)
    swish = gate_lin * sigmoid_gate
    active = (swish * upward).astype(jnp.bfloat16)
    output = (middle + jnp.dot(active, down_full, preferred_element_type=jnp.float32)).astype(
        jnp.bfloat16
    )
    ffn_scale, gate_full, up_full, down_full = (
        lax.all_gather(ffn_gain, ("dp", "seq"), axis=0, tiled=True),
        lax.all_gather(w_gate, ("dp", "seq"), axis=0, tiled=True),
        lax.all_gather(w_up, ("dp", "seq"), axis=0, tiled=True),
        lax.all_gather(w_down, ("dp", "seq"), axis=0, tiled=True),
    )
    d_active = lax.dot_general(
        cotangent, down_full, CONTRACT_COLS, preferred_element_type=jnp.float32
    )
    d_gate = (d_active * upward * (sigmoid_gate * (1.0 + gate_lin * (1.0 - sigmoid_gate)))).astype(
        jnp.bfloat16
    )
    d_up = (d_active * swish).astype(jnp.bfloat16)
    d_normed_mid = lax.dot_general(
        d_gate, gate_full, CONTRACT_COLS, preferred_element_type=jnp.float32
    )
    d_normed_mid = d_normed_mid + lax.dot_general(
        d_up, up_full, CONTRACT_COLS, preferred_element_type=jnp.float32
    )
    d_middle_norm, ffn_gain_part = norm_back(d_normed_mid, middle, ffn_scale.astype(jnp.float32))
    d_middle = cotangent.astype(jnp.float32) + d_middle_norm
    d_branch = d_middle.astype(jnp.bfloat16)
    attn_scale, query_full, key_full, value_full, out_full = (
        lax.all_gather(attn_gain, ("dp", "seq"), axis=0, tiled=True),
        lax.all_gather(w_query, ("dp", "seq"), axis=0, tiled=True),
        lax.all_gather(key_projection_weight, ("dp", "seq"), axis=0, tiled=True),
        lax.all_gather(value_projection_weight, ("dp", "seq"), axis=0, tiled=True),
        lax.all_gather(w_out, ("dp", "seq"), axis=0, tiled=True),
    )
    d_attended = lax.dot_general(
        d_branch, out_full, CONTRACT_COLS, preferred_element_type=jnp.float32
    ).astype(jnp.bfloat16)
    d_mixture = lax.all_to_all(d_attended, "seq", split_axis=1, concat_axis=0, tiled=True)
    d_q_heads, d_k_heads, d_v_heads = attend_back(
        q_heads, k_heads, v_heads, d_mixture, log_total, all_places, all_docs
    )
    d_q_sent, key_sent_gradient, d_v_sent = (
        lax.all_to_all(d_q_heads, "seq", split_axis=0, concat_axis=1, tiled=True),
        lax.all_to_all(d_k_heads, "seq", split_axis=0, concat_axis=1, tiled=True),
        lax.all_to_all(d_v_heads, "seq", split_axis=0, concat_axis=1, tiled=True),
    )
    d_q_linear, q_gain_part = head_backward_pass(
        d_q_sent, q_linear, q_scale, cosine_table, sine_table, QUERY_HEADS
    )
    key_linear_gradient, key_gain_piece = head_backward_pass(
        key_sent_gradient,
        key_linear_output,
        key_norm_scale,
        cosine_table,
        sine_table,
        KEY_VALUE_HEADS,
    )
    d_normed = lax.dot_general(
        d_q_linear, query_full, CONTRACT_COLS, preferred_element_type=jnp.float32
    )
    d_normed = d_normed + lax.dot_general(
        key_linear_gradient, key_full, CONTRACT_COLS, preferred_element_type=jnp.float32
    )
    d_normed = d_normed + lax.dot_general(
        d_v_sent, value_full, CONTRACT_COLS, preferred_element_type=jnp.float32
    )
    d_source_norm, attn_gain_part = norm_back(d_normed, source, attn_scale.astype(jnp.float32))
    input_grad = d_middle + d_source_norm
    attn_columns = jnp.concatenate([d_q_linear, key_linear_gradient, d_v_sent], axis=1)
    ffn_columns = jnp.concatenate([d_gate, d_up], axis=1)
    left = normalized_input
    first_part = lax.dot_general(
        left, attn_columns, CONTRACT_ROWS, preferred_element_type=jnp.float32
    )
    second_part = lax.dot_general(
        normed_mid, ffn_columns, CONTRACT_ROWS, preferred_element_type=jnp.float32
    )
    width_sums = lax.psum_scatter(
        jnp.concatenate([first_part, second_part], axis=1),
        ("dp", "seq"),
        scatter_dimension=0,
        tiled=True,
    )
    left = attended
    out_grad = lax.psum_scatter(
        lax.dot_general(left, d_branch, CONTRACT_ROWS, preferred_element_type=jnp.float32),
        ("dp", "seq"),
        scatter_dimension=0,
        tiled=True,
    )
    left = active
    down_grad = lax.psum_scatter(
        lax.dot_general(left, cotangent, CONTRACT_ROWS, preferred_element_type=jnp.float32),
        ("dp", "seq"),
        scatter_dimension=0,
        tiled=True,
    )
    attn_gain_grad, ffn_gain_grad = (
        lax.psum_scatter(attn_gain_part, ("dp", "seq"), scatter_dimension=0, tiled=True),
        lax.psum_scatter(ffn_gain_part, ("dp", "seq"), scatter_dimension=0, tiled=True),
    )
    q_gain_grad, k_gain_grad = lax.psum((q_gain_part, key_gain_piece), ("dp", "seq"))
    q_cols = QUERY_HEADS * HEAD_SIZE
    kv_cols = KEY_VALUE_HEADS * HEAD_SIZE
    query_grad = width_sums[:, :q_cols]
    key_grad = width_sums[:, q_cols : q_cols + kv_cols]
    value_grad = width_sums[:, q_cols + kv_cols : q_cols + 2 * kv_cols]
    gate_grad = width_sums[:, q_cols + 2 * kv_cols : q_cols + 2 * kv_cols + FF]
    up_grad = width_sums[:, q_cols + 2 * kv_cols + FF :]
    return (
        output,
        input_grad,
        attn_gain_grad,
        query_grad,
        key_grad,
        value_grad,
        q_gain_grad,
        k_gain_grad,
        out_grad,
        ffn_gain_grad,
        gate_grad,
        up_grad,
        down_grad,
    )


def solution(mesh):
    placed = (
        P(("dp", "seq"), None),
        P("dp", None),
        P(("dp", "seq"), None),
        P(("dp", "seq")),
        P(("dp", "seq"), None),
        P(("dp", "seq"), None),
        P(("dp", "seq"), None),
        P(),
        P(),
        P(("dp", "seq"), None),
        P(("dp", "seq")),
        P(("dp", "seq"), None),
        P(("dp", "seq"), None),
        P(("dp", "seq"), None),
    )
    return jax.shard_map(
        on_device,
        mesh=mesh,
        in_specs=placed,
        out_specs=(
            P(("dp", "seq"), None),
            P(("dp", "seq"), None),
            P(("dp", "seq")),
            P(("dp", "seq"), None),
            P(("dp", "seq"), None),
            P(("dp", "seq"), None),
            P(),
            P(),
            P(("dp", "seq"), None),
            P(("dp", "seq")),
            P(("dp", "seq"), None),
            P(("dp", "seq"), None),
            P(("dp", "seq"), None),
        ),
        check_vma=False,
    )
```

profile of v0, /device:TPU:0, one launch (start us, length us, event | category | flops | bytes accessed | tf_op | source)
XLA Modules:
  0.0 1508.7 jit_solution(15136424277290650335)
XLA Ops:
  14.9 42.0 %all-reduce.5 = (bf16[1024]{0:T(1024)(128)(2,1)S(1)}, bf16[1024]{0:T(1024)(128)(2,1)S(1)}) all-reduce(bf16[1024]{0:T(1024)(128)(2,1)S(1)} %dynamic-update-slice, bf16[1024]{0:T(1024)(128)(2,1)S(1)} %dynamic-update-slice.1), channel_id=1, replica_groups=mesh['dp'=8,'seq'=4] {'dp','seq'}, use_global_device_ids=true, to_apply=%add | all-reduce | flops 2048 | bytes 8192
  61.1 6.3 all-gather.12.cloned.1.call-done
  73.2 49.8 %all-gather.10.cloned.1.call-done = bf16[1024,512]{1,0:T(8,128)(2,1)} async-done(((bf16[32,512]{1,0:T(8,128)(2,1)}), bf16[1024,512]{1,0:T(8,128)(2,1)}) %all-gather.10.cloned.1.call-update) | async-done | bytes 1048592 | tf_op jit(solution)/shard_map/all_gather | solution.py:205
  135.0 46.2 %all-gather.8.cloned.1.call-done = bf16[1024,1024]{1,0:T(8,128)(2,1)} async-done(((bf16[32,1024]{1,0:T(8,128)(2,1)}), bf16[1024,1024]{1,0:T(8,128)(2,1)}) %all-gather.8.cloned.1.call-update) | async-done | bytes 2097168 | tf_op jit(solution)/shard_map/all_gather | solution.py:204
  193.1 4.1 all-to-all-start.1
  203.3 3.8 all-to-all-start
  208.9 8.4 all-to-all-done
  218.1 15.2 %while.28 = (s32[]{:T(128)}, bf16[2,512,2,2,64]{1,4,3,2,0:T(8,128)(2,1)S(1)}, f32[2,2,2,512]{3,2,1,0:T(2,128)S(1)}, s32[2,512]{1,0:T(2,128)S(1)}, s32[1024]{0:T(...) while((s32[]{:T(128)}, ...), condition=%wide.region_8.9_spmd.clone, body=%wide.region_5.8_spmd.clone.sunk | while | flops 563738624 | bytes 28393596 | solution.py:106
  234.9 4.0 all-to-all-start.3
  240.4 7.3 all-to-all-done.3
  250.5 73.6 %all-gather.18.cloned.1.call-done = bf16[1024,4608]{1,0:T(8,128)(2,1)} async-done(((bf16[32,4608]{1,0:T(8,128)(2,1)}), bf16[1024,4608]{1,0:T(8,128)(2,1)}) %all-gather.18.cloned.1.call-update) | async-done | bytes 9437200 | tf_op jit(solution)/shard_map/all_gather | solution.py:231
  324.1 7.9 fusion.105
  332.0 75.5 %all-gather.16.cloned.1.call-done = bf16[1024,4608]{1,0:T(8,128)(2,1)} async-done(((bf16[32,4608]{1,0:T(8,128)(2,1)}), bf16[1024,4608]{1,0:T(8,128)(2,1)}) %all-gather.16.cloned.1.call-update) | async-done | bytes 9437200 | tf_op jit(solution)/shard_map/all_gather | solution.py:230
  407.5 7.9 fusion.104
  415.5 75.6 %all-gather.20.cloned.1.call-done = bf16[4608,1024]{1,0:T(8,128)(2,1)} async-done(((bf16[144,1024]{1,0:T(8,128)(2,1)}), bf16[4608,1024]{1,0:T(8,128)(2,1)}) %all-gather.20.cloned.1.call-update) | async-done | bytes 9437200 | tf_op jit(solution)/shard_map/all_gather | solution.py:232
  491.1 13.5 multiply_convert_fusion
  507.2 6.2 multiply_reduce_fusion
  516.5 3.6 all-to-all-start.4
  520.2 8.8 all-to-all-done.4
  531.6 26.4 %while.29 = (s32[]{:T(128)}, f32[1024,2,64]{0,2,1:T(8,128)S(1)}, f32[1024,2,64]{0,2,1:T(8,128)}, bf16[2,512,2,2,64]{1,4,3,2,0:T(8,128)(2,1)}, bf16[2,512,2,2,64]...) while((s32[]{:T(128)}, f32[1024,2,64]{0,2,1:T(8,128)S(1)}, ...), condition=%wide.region_13.14_spmd.clone, body=%wide.region_11.13_spmd.clone.sunk | while | flops 1375991808 | bytes 77930784 | solution.py:166
  562.5 17.3 %fusion.58 = f32[1024,9216]{1,0:T(8,128)} fusion(bf16[256,1024]{1,0:T(8,128)(2,1)S(1)} %multiply_convert_fusion.4, bf16[256,4608]{1,0:T(8,128)(2,1)} %copy-done.28, bf16[256,4608]{1,0:T(8,128)(2,1)} %copy-done.29), kind=kOutput, calls=%fused_computation.69 | convolution fusion | flops 4841275392 | bytes 42991616 | tf_op jit(solution)/shard_map/dot_general | solution.py:312
  587.2 4.8 all-to-all-done.7
  592.0 4.1 all-to-all-start.5
  620.3 4.7 fusion.76
  625.0 29.7 %pad_maximum_fusion = f32[1024,11264]{1,0:T(8,128)} fusion(f32[1024,9216]{1,0:T(8,128)} %fusion.58, f32[1024,2048]{1,0:T(8,128)} %fusion.76), kind=kLoop, calls=%fused_computation.68 | loop fusion | flops 11534336 | bytes 92274688 | tf_op jit(solution)/shard_map/concatenate | solution.py:316
  655.9 3.8 fusion.87
  660.1 11.1 fusion.108
  671.2 8.4 fusion.67
  688.5 43.9 %all-reduce.4 = (f32[1024]{0:T(1024)S(1)}, f32[64]{0:T(128)}, f32[64]{0:T(128)}, f32[1024]{0:T(1024)S(1)}) all-reduce(f32[1024]{0:T(1024)S(1)} %get-tuple-element.308, f32[64]{0:T(128)S(1)} %reduce_sum.177, f32[64]{0:T(128)S(1)} %reduce_sum.180, f32[1024]{0:T(1024)S(1)} %copy-done.54), channel_id=2, replica_groups=mesh['dp'=8,'seq'=4] {'dp','seq'}, use_global_device_ids=true, to_apply=%region_18.19.clone | all-reduce | flops 2176 | bytes 17408
  734.8 405.0 %reduce-scatter.4.cloned.1.call-done = f32[32,11264]{1,0:T(8,128)} async-done(((f32[1024,11264]{1,0:T(8,128)}), f32[32,11264]{1,0:T(8,128)}) %reduce-scatter.4.cloned.1.call-update) | async-done | bytes 1441808 | tf_op jit(solution)/shard_map/reduce_scatter | solution.py:315
  1145.3 146.5 %reduce-scatter.6.cloned.1.call-done = f32[32,1024]{1,0:T(8,128)} async-done(((f32[1024,1024]{1,0:T(8,128)}), f32[32,1024]{1,0:T(8,128)}) %reduce-scatter.6.cloned.1.call-update) | async-done | bytes 131088 | tf_op jit(solution)/shard_map/reduce_scatter | solution.py:322
  1291.8 209.6 %reduce-scatter.8.cloned.1.call-done = f32[144,1024]{1,0:T(8,128)} async-done(((f32[4608,1024]{1,0:T(8,128)}), f32[144,1024]{1,0:T(8,128)}) %reduce-scatter.8.cloned.1.call-update) | async-done | bytes 589840 | tf_op jit(solution)/shard_map/reduce_scatter | solution.py:329
  (308 shorter events, 159.5 us)
Async XLA Ops:
  7.2 53.7 %copy-start.2 = (bf16[256,1024]{1,0:T(8,128)(2,1)S(1)}, bf16[256,1024]{1,0:T(8,128)(2,1)}, u32[]{:S(2)}) copy-start(bf16[256,1024]{1,0:T(8,128)(2,1)} %param.18) | copy-start | bytes 1572868
  7.2 60.2 %all-gather.12.cloned.1.call-start = ((), (), s32[]{:S(2)}) async-start(), calls=%async_computation.13 | async-start | bytes 1081344 | tf_op jit(solution)/shard_map/all_gather | solution.py:206
  7.9 115.1 %all-gather.10.cloned.1.call-start = ((), (), s32[]{:S(2)}) async-start(), calls=%async_computation.12 | async-start | bytes 1081344 | tf_op jit(solution)/shard_map/all_gather | solution.py:205
  8.7 172.6 %all-gather.8.cloned.1.call-start = ((), (), s32[]{:S(2)}) async-start(), calls=%async_computation.11 | async-start | bytes 2162688 | tf_op jit(solution)/shard_map/all_gather | solution.py:204
  9.4 231.0 %all-gather.14.cloned.1.call-start = ((), (), s32[]{:S(2)}) async-start(), calls=%async_computation.14 | async-start | bytes 2162688 | tf_op jit(solution)/shard_map/all_gather | solution.py:207
  10.0 314.1 %all-gather.18.cloned.1.call-start = ((), (), s32[]{:S(2)}) async-start(), calls=%async_computation.16 | async-start | bytes 9732096 | tf_op jit(solution)/shard_map/all_gather | solution.py:231
  10.6 396.9 %all-gather.16.cloned.1.call-start = ((), (), s32[]{:S(2)}) async-start(), calls=%async_computation.15 | async-start | bytes 9732096 | tf_op jit(solution)/shard_map/all_gather | solution.py:230
  11.1 479.9 %all-gather.20.cloned.1.call-start = ((), (), s32[]{:S(2)}) async-start(), calls=%async_computation.17 | async-start | bytes 9732096 | tf_op jit(solution)/shard_map/all_gather | solution.py:232
  12.6 177.5 %copy-start.55 = (f32[64]{0:T(128)}, f32[64]{0:T(128)S(1)}, u32[]{:S(2)}) copy-start(f32[64]{0:T(128)S(1)} %convert_element_type.153) | copy-start | bytes 772
  13.2 115.7 %copy-start.56 = (f32[64]{0:T(128)}, f32[64]{0:T(128)S(1)}, u32[]{:S(2)}) copy-start(f32[64]{0:T(128)S(1)} %convert_element_type.156) | copy-start | bytes 772
  56.9 124.4 %copy-start.43 = (f32[1024]{0:T(1024)}, f32[1024]{0:T(1024)S(1)}, u32[]{:S(2)}) copy-start(f32[1024]{0:T(1024)S(1)} %convert_element_type.151) | copy-start | bytes 12292
  57.6 74.4 %copy-start.53 = (f32[512]{0:T(512)}, f32[512]{0:T(512)S(1)}, u32[]{:S(2)}) copy-start(f32[512]{0:T(512)S(1)} %mul.453) | copy-start | bytes 6148
  58.3 138.8 %copy-start.51 = (f32[1024]{0:T(1024)}, f32[1024]{0:T(1024)S(1)}, u32[]{:S(2)}) copy-start(f32[1024]{0:T(1024)S(1)} %mul.430) | copy-start | bytes 12292
  59.3 131.1 %copy-start.34 = (f32[256,64]{0,1:T(8,128)}, f32[256,64]{0,1:T(8,128)S(1)}, u32[]{:S(2)}) copy-start(f32[256,64]{0,1:T(8,128)S(1)} %get-tuple-element.390) | copy-start | bytes 196612
  60.4 71.6 %copy-start.14 = (f32[256,512]{1,0:T(8,128)}, f32[256,512]{1,0:T(8,128)S(1)}, u32[]{:S(2)}) copy-start(f32[256,512]{1,0:T(8,128)S(1)} %copy.197) | copy-start | bytes 1572868
  60.5 62.5 %copy-start.11 = (f32[256,16,64]{0,2,1:T(8,128)}, f32[256,16,64]{0,2,1:T(8,128)S(1)}, u32[]{:S(2)}) copy-start(f32[256,16,64]{0,2,1:T(8,128)S(1)} %mul.439) | copy-start | bytes 3145732
  60.9 136.3 %copy-start.9 = (f32[256,1024]{1,0:T(8,128)}, f32[256,1024]{1,0:T(8,128)S(1)}, u32[]{:S(2)}) copy-start(f32[256,1024]{1,0:T(8,128)S(1)} %copy.191) | copy-start | bytes 3145732
  61.1 120.1 %copy-start.49 = (f32[256]{0:T(256)}, f32[256]{0:T(256)S(1)}, u32[]{:S(2)}) copy-start(f32[256]{0:T(256)S(1)} %add_rsqrt_fusion.3) | copy-start | bytes 3076
  69.8 123.3 %all-to-all-start.2 = ((bf16[256,4,128]{2,0,1:T(8,128)(2,1)}), bf16[256,4,128]{2,0,1:T(8,128)(2,1)S(1)}, u32[]{:S(2)}, u32[]{:S(2)}) async-start(bf16[256,4,128]{2,0,1:T(8,128)(2,1)} %bitcast.357), calls=%async_computation.2 | async-start | bytes 524288 | tf_op jit(solution)/shard_map/all_to_all | solution.py:223
  126.8 57.7 %copy-start.47 = (f32[256,8]{0,1:T(8,128)}, f32[256,8]{0,1:T(8,128)S(1)}, u32[]{:S(2)}) copy-start(f32[256,8]{0,1:T(8,128)S(1)} %add_rsqrt_fusion.1) | copy-start | bytes 24580
  193.1 10.2 all-to-all-start.1
  203.3 14.0 all-to-all-start
  234.9 12.8 all-to-all-start.3
  250.3 263.1 %copy-start.10 = (f32[256,1024]{1,0:T(8,128)}, f32[256,1024]{1,0:T(8,128)S(1)}, u32[]{:S(2)}) copy-start(f32[256,1024]{1,0:T(8,128)S(1)} %get-tuple-element.392) | copy-start | bytes 3145732
  332.0 159.1 %copy-start.30 = (bf16[256,1024]{1,0:T(8,128)(2,1)S(1)}, bf16[256,1024]{1,0:T(8,128)(2,1)}, u32[]{:S(2)}) copy-start(bf16[256,1024]{1,0:T(8,128)(2,1)} %param.20) | copy-start | bytes 1572868
  516.5 12.4 all-to-all-start.4
  558.9 23.7 %all-to-all-start.6 = ((bf16[4,256,128]{1,2,0:T(8,128)(2,1)}), bf16[4,256,128]{1,2,0:T(8,128)(2,1)S(1)}, u32[]{:S(2)}, u32[]{:S(2)}) async-start(bf16[4,256,128]{1,2,0:T(8,128)(2,1)} %copy.217), calls=%async_computation.6 | async-start | bytes 524288 | tf_op jit(solution)/shard_map/all_to_all | solution.py:281
  582.6 9.4 all-to-all-start.7
  592.0 13.1 all-to-all-start.5
  596.1 543.7 %reduce-scatter.4.cloned.1.call-start = ((), (), s32[]{:S(2)}) async-start(), calls=%async_computation.18 | async-start | bytes 47579136 | tf_op jit(solution)/shard_map/reduce_scatter | solution.py:315
  654.7 637.0 %reduce-scatter.6.cloned.1.call-start = ((), (), s32[]{:S(2)}) async-start(), calls=%async_computation.19 | async-start | bytes 4325376 | tf_op jit(solution)/shard_map/reduce_scatter | solution.py:322
  659.8 841.6 %reduce-scatter.8.cloned.1.call-start = ((), (), s32[]{:S(2)}) async-start(), calls=%async_computation.20 | async-start | bytes 19464192 | tf_op jit(solution)/shard_map/reduce_scatter | solution.py:329
  (48 other events, 342.7 us)
Sparse Core Ops, SparseCore 0:
  10.9 56.4 all-gather.11
  70.2 52.7 all-gather.9
  125.9 55.3 all-gather.7
  184.0 56.3 all-gather.13
  243.1 80.8 all-gather.17
  326.8 80.6 all-gather.15
  410.4 80.6 all-gather.19
  654.9 484.9 reduce-scatter.3
  1142.7 149.0 reduce-scatter.5
  1298.6 202.7 reduce-scatter.7
where the time goes:
time: 1520 us; the launch traced here: 1510 us
  waiting for transfers between devices  1130 us (74%)
  matrix products  128 us (8%)
  blocking collectives  85.9 us (6%)
  other arithmetic  66.3 us (4%)
  local copies, waits for them, and re-layouts  53.8 us (4%)
  starting transfers between devices  30.7 us (2%)
  between operations  15.7 us (1%)
    reduce_scatter x1, waiting for transfers between devices, on_device(): lax.psum_scatter(jnp.concatenate([first_part, second_part], axis=1), ('dp...  405 us
    reduce_scatter x1, waiting for transfers between devices, on_device(): lax.psum_scatter(lax.dot_general(left, cotangent, CONTRACT_ROWS, preferre...  210 us
    reduce_scatter x1, waiting for transfers between devices, on_device(): lax.psum_scatter(lax.dot_general(left, d_branch, CONTRACT_ROWS, preferred...  146 us
    unnamed x2, blocking collectives  85.9 us
    all_gather x1, waiting for transfers between devices, on_device(): lax.all_gather(w_down, ('dp', 'seq'), axis=0, tiled=True)  75.6 us
    all_gather x1, waiting for transfers between devices, on_device(): lax.all_gather(w_gate, ('dp', 'seq'), axis=0, tiled=True)  75.5 us
    all_gather x1, waiting for transfers between devices, on_device(): lax.all_gather(w_up, ('dp', 'seq'), axis=0, tiled=True)  73.6 us
    all_gather x1, waiting for transfers between devices, on_device(): lax.all_gather(key_projection_weight, ('dp', 'seq'), axis=0, tiled=True)  49.8 us
  transfers between devices with their start and end apart: 18, of which 16 were waited for; matrix products, arithmetic and copies ran while one was open for 9% of the time, Pallas kernels for 0%

commit v1 on v0

--- a/solution.py
+++ b/solution.py
@@ -1,6 +1,9 @@
 import jax
 import jax.numpy as jnp
+import numpy as np
 from jax import lax
+from jax.experimental import pallas as pl
+from jax.experimental.pallas import tpu as pltpu
 from jax.sharding import PartitionSpec as P
 
 QUERY_HEADS = 16
@@ -361,7 +364,977 @@
     )
 
 
+BF = jnp.bfloat16
+F32 = jnp.float32
+MESH = pl.DeviceIdType.MESH
+SEQ = 4
+PLANES = 4
+TOK = 256
+WIDTH = 1024
+ROW = 1024
+OWN_Q = 256
+OWN_K = 128
+QKV = 512
+FF_OWN = 1152
+FF_SHARD = 144
+HIDDEN_TWO = 2304
+DOWN_A = 64
+DOWN_B = 80
+
+
+def flip(value, bit):
+    return value + bit - 2 * bit * lax.rem(lax.div(value, bit), 2)
+
+
+def dot(left, right):
+    return lax.dot_general(left, right, (((1,), (0,)), ((), ())), preferred_element_type=F32)
+
+
+def dot_nt(left, right):
+    return lax.dot_general(left, right, (((1,), (1,)), ((), ())), preferred_element_type=F32)
+
+
+def dot_tn(left, right):
+    return lax.dot_general(left, right, (((0,), (0,)), ((), ())), preferred_element_type=F32)
+
+
+class Links:
+    def __init__(self, send_sems, recv_sems):
+        self.send_sems, self.recv_sems = send_sems, recv_sems
+        self.used = 0
+        self.open = []
+        self.dp = lax.axis_index("dp")
+        self.s = lax.axis_index("seq")
+        self.s1 = flip(self.s, 1)
+        self.s2 = flip(self.s, 2)
+        self.s3 = flip(self.s1, 2)
+        self.others = (self.s1, self.s2, self.s3)
+        self.y = lax.rem(self.dp, 2)
+        self.z = lax.div(self.dp, 2)
+        self.y_peer = flip(self.dp, 1)
+        z1 = flip(self.z, 1)
+        self.planes = (z1, flip(self.z, 2), flip(z1, 2))
+        self.z_peers = tuple(2 * z + self.y for z in self.planes)
+
+    def greet(self, semaphore, partners):
+        for place in partners:
+            pl.semaphore_signal(semaphore, inc=1, device_id=place, device_id_type=MESH)
+
+    def column(self):
+        return [(p, self.s) for p in (self.y_peer,) + self.z_peers]
+
+    def everyone(self):
+        return [(self.dp, s) for s in self.others] + self.column()
+
+    def plan(self, src, dst, dp=None, s=None):
+        n = self.used
+        self.used += 1
+        copy = pltpu.make_async_remote_copy(
+            src_ref=src,
+            dst_ref=dst,
+            send_sem=self.send_sems.at[n],
+            recv_sem=self.recv_sems.at[n],
+            device_id=(self.dp if dp is None else dp, self.s if s is None else s),
+            device_id_type=MESH,
+        )
+        return copy
+
+    def push(self, src, dst, dp=None, s=None, when=None):
+        copy = self.plan(src, dst, dp, s)
+        if when is None:
+            copy.start()
+        else:
+            pl.when(when)(copy.start)
+        self.open.append((copy, when))
+        return copy
+
+    def settle(self, copies):
+        for copy in copies:
+            copy.wait_send()
+        self.open = [item for item in self.open if all(item[0] is not copy for copy in copies)]
+
+    def drain(self):
+        for copy, when in self.open:
+            if when is None:
+                copy.wait_send()
+            else:
+                pl.when(when)(copy.wait_send)
+        self.open = []
+
+
+class Line:
+    def __init__(self, links, view):
+        self.links, self.view = links, view
+        self.hops = []
+
+    def pass_on(self, step):
+        l = self.links
+        below, above = l.z - step, l.z + step
+        low = self.view(jnp.maximum(below, 0))
+        high = self.view(jnp.minimum(above, PLANES - 1))
+        up = l.push(
+            low, low, dp=jnp.minimum(l.dp + 2, 2 * PLANES - 1), when=(below >= 0) & (l.z < PLANES - 1)
+        )
+        down = l.push(high, high, dp=jnp.maximum(l.dp - 2, 0), when=(above <= PLANES - 1) & (l.z > 0))
+        self.hops.append((up, down))
+
+    def start(self):
+        self.pass_on(0)
+
+    def step(self, k):
+        l = self.links
+        below, above = l.z - 1 - k, l.z + 1 + k
+        from_below, from_above = below >= 0, above <= PLANES - 1
+        pl.when(from_below)(self.hops[k][0].wait_recv)
+        pl.when(from_above)(self.hops[k][1].wait_recv)
+        if k < PLANES - 2:
+            self.pass_on(k + 1)
+        return [
+            (from_below, self.view(jnp.maximum(below, 0))),
+            (from_above, self.view(jnp.minimum(above, PLANES - 1))),
+        ]
+
+
+class Gather:
+    def __init__(self, links, view):
+        self.links = links
+        self.line = Line(links, lambda z: view(2 * z + links.y))
+        self.own = view(links.dp)
+        self.over_y = []
+
+    def start_y(self):
+        self.over_y.append((None, self.links.push(self.own, self.own, dp=self.links.y_peer)))
+
+    def start_z(self):
+        self.line.start()
+
+    def step(self, k):
+        for when, block in self.line.step(k):
+            copy = self.links.push(block, block, dp=self.links.y_peer, when=when)
+            self.over_y.append((when, copy))
+
+    def finish(self):
+        for when, copy in self.over_y:
+            if when is None:
+                copy.wait_recv()
+            else:
+                pl.when(when)(copy.wait_recv)
+
+
+class PairGather:
+    def __init__(self, links, view):
+        self.links = links
+        self.near = Line(links, lambda z: view(2 * z + links.y))
+        self.far = Line(links, lambda z: view(2 * z + 1 - links.y))
+        self.own = view(links.dp)
+
+    def start_y(self):
+        self.over_y = self.links.push(self.own, self.own, dp=self.links.y_peer)
+
+    def start_z(self):
+        self.near.start()
+
+    def join(self):
+        self.over_y.wait_recv()
+        self.far.start()
+
+    def step(self, k):
+        self.near.step(k)
+        self.far.step(k)
+
+
+class Chain:
+    def __init__(self, links, view, slots):
+        self.links, self.view, self.slots = links, view, slots
+        self.up, self.down = {}, {}
+
+    def start(self):
+        l = self.links
+        last = PLANES - 1
+        for d in range(PLANES):
+            if d > 0:
+                self.up[d] = l.plan(self.view(d), self.slots(d), dp=jnp.minimum(l.dp + 2, 2 * last + 1))
+            if d < last:
+                place = jnp.where(l.z == d + 1, PLANES, d)
+                self.down[d] = l.plan(self.view(d), self.slots(place), dp=jnp.maximum(l.dp - 2, 0))
+
+    def add(self, d, copy):
+        copy.wait_recv()
+        block = self.view(d)
+        block[...] = (block[...].astype(F32) + self.slots(d)[...].astype(F32)).astype(BF)
+
+    def step(self, j):
+        last = PLANES - 1
+
+        @pl.when(self.links.z == j)
+        def _():
+            for d in range(last, j, -1):
+                if j > 0:
+                    self.add(d, self.up[d])
+                self.up[d].start()
+
+        @pl.when(self.links.z == last - j)
+        def _():
+            for d in range(last - j):
+                if j > 0:
+                    self.add(d, self.down[d])
+                self.down[d].start()
+
+        for d in range(PLANES):
+            if d > j:
+                self.links.open.append((self.up[d], self.links.z == j))
+            if d < last - j:
+                self.links.open.append((self.down[d], self.links.z == last - j))
+
+    def total(self):
+        l = self.links
+        for d in range(PLANES):
+            if d > 0:
+                pl.when(l.z == d)(self.up[d].wait_recv)
+            if d < PLANES - 1:
+                pl.when(l.z == d)(self.down[d].wait_recv)
+        own = self.view(l.z)[...].astype(F32)
+        below = jnp.where(l.z > 0, self.slots(l.z)[...].astype(F32), 0.0)
+        above = jnp.where(l.z < PLANES - 1, self.slots(PLANES)[...].astype(F32), 0.0)
+        return own + (below + above)
+
+
+class Scatter:
+    def __init__(self, links, view, y_slots, z_slots):
+        self.links, self.view, self.y_slots = links, view, y_slots
+        self.chain = Chain(links, lambda z: view(2 * z + links.y), z_slots)
+
+    def start(self):
+        l = self.links
+        self.order = [jnp.where(l.z < PLANES // 2, PLANES - 1 - k, k) for k in range(PLANES)]
+        self.over_y = [
+            l.push(self.view(2 * d + 1 - l.y), self.y_slots(k), dp=l.y_peer) for k, d in enumerate(self.order)
+        ]
+        self.chain.start()
+
+    def join(self):
+        for k, copy in enumerate(self.over_y):
+            copy.wait_recv()
+            block = self.view(2 * self.order[k] + self.links.y)
+            block[...] = (block[...].astype(F32) + self.y_slots(k)[...].astype(F32)).astype(BF)
+
+    def step(self, j):
+        self.chain.step(j)
+
+    def total(self):
+        return self.chain.total()
+
+
+class PairScatter:
+    def __init__(self, links, view, y_slot, near_slots, far_slots):
+        self.links, self.view, self.y_slot = links, view, y_slot
+        self.near = Chain(links, lambda z: view(2 * z + links.y), near_slots)
+        self.far = Chain(links, lambda z: view(2 * z + 1 - links.y), far_slots)
+
+    def start(self):
+        self.far.start()
+        self.near.start()
+
+    def step(self, j):
+        self.far.step(j)
+        self.near.step(j)
+
+    def cross(self):
+        l = self.links
+        block = self.view(2 * l.z + 1 - l.y)
+        block[...] = self.far.total().astype(BF)
+        self.over_y = l.push(block, self.y_slot, dp=l.y_peer)
+
+    def total(self):
+        own = self.near.total()
+        self.over_y.wait_recv()
+        return own + self.y_slot[...].astype(F32)
+
+
+class RowSum:
+    def __init__(self, links, slots):
+        self.links, self.slots = links, slots
+
+    def hand_over(self, src):
+        self.first = self.links.push(src, self.slots.at[0], s=self.links.s1)
+
+    def cross(self, src):
+        self.first.wait_recv()
+        src[...] = (src[...].astype(F32) + self.slots[0].astype(F32).reshape(src.shape)).astype(BF)
+        self.second = self.links.push(src, self.slots.at[1], s=self.links.s2)
+
+    def near(self, src):
+        self.third = self.links.push(src, self.slots.at[2], s=self.links.s1)
+
+    def total(self, own):
+        self.third.wait_recv()
+        self.second.wait_recv()
+        return own + self.slots[1].astype(F32).reshape(own.shape) + self.slots[2].astype(F32).reshape(own.shape)
+
+
+def lane_masks(rows):
+    lane = lax.broadcasted_iota(jnp.int32, (rows, 128), 1)
+    return lane < 64, lax.rem(lane, 64) < 32
+
+
+def turned(values, low):
+    return jnp.where(low, -pltpu.roll(values, 96, 1), pltpu.roll(values, 32, 1))
+
+
+def unturned(values, low):
+    return jnp.where(low, pltpu.roll(values, 96, 1), -pltpu.roll(values, 32, 1))
+
+
+def per_head_mean(values, first):
+    left = jnp.sum(jnp.where(first, values, 0.0), axis=-1, keepdims=True)
+    right = jnp.sum(jnp.where(first, 0.0, values), axis=-1, keepdims=True)
+    return jnp.where(first, left, right) * (1.0 / HEAD_SIZE)
+
+
+def norm_rope(values, gain, cosine, sine, first, low):
+    normed = values * lax.rsqrt(per_head_mean(values * values, first) + EPS) * gain
+    return normed * cosine + turned(normed, low) * sine
+
+
+def norm_rope_back(upstream, values, gain, cosine, sine, first, low):
+    d_normed = upstream * cosine + unturned(upstream * sine, low)
+    inverse = lax.rsqrt(per_head_mean(values * values, first) + EPS)
+    unit = values * inverse
+    scaled = d_normed * gain
+    d_values = inverse * (scaled - unit * per_head_mean(scaled * unit, first))
+    return d_values, jnp.sum(d_normed * unit, axis=0, keepdims=True)
+
+
+def allowed_block(r, block, keys):
+    query = lax.broadcasted_iota(jnp.int32, (TOK, keys), 0) + block * TOK
+    key = lax.broadcasted_iota(jnp.int32, (TOK, keys), 1)
+    place = lax.broadcasted_iota(jnp.int32, (TOK, 1), 0) + block * TOK
+    begin = jnp.zeros((TOK, 1), jnp.int32)
+    for k in range(4):
+        start = r.doc_starts[0, k]
+        begin = jnp.maximum(begin, jnp.where(place >= start, start, 0))
+    return (key <= query) & (key >= begin)
+
+
+SCORE_SCALE = HEAD_SIZE ** (-0.5)
+
+
+def attention_block(r, pair, block):
+    keys = (block + 1) * TOK
+    rows = pl.ds(block * TOK, TOK)
+    queries = r.q_heads[pair, :, rows, :].reshape(2 * TOK, HEAD_SIZE)
+    scores = dot_nt(queries, r.k_heads[pair, :keys, :]).reshape(2, TOK, keys) * SCORE_SCALE
+    scores = jnp.where(allowed_block(r, block, keys)[None], scores, MASKED)
+    top = jnp.max(scores, axis=-1, keepdims=True)
+    weights = jnp.exp(scores - top)
+    total = jnp.sum(weights, axis=-1, keepdims=True)
+    mixed = dot(weights.astype(BF).reshape(2 * TOK, keys), r.v_heads[pair, :keys, :])
+    mixed = mixed.reshape(2, TOK, HEAD_SIZE) / total
+    log_total = top + jnp.log(total)
+    r.log_total[rows, 2 * pair : 2 * pair + 1] = log_total[0]
+    r.log_total[rows, 2 * pair + 1 : 2 * pair + 2] = log_total[1]
+    r.att_own[block, :, pair * 128 : (pair + 1) * 128] = jnp.concatenate(
+        [mixed[0], mixed[1]], axis=-1
+    ).astype(BF)
+
+
+def attention_block_back(r, pair, block):
+    keys = (block + 1) * TOK
+    rows = pl.ds(block * TOK, TOK)
+    queries = r.q_heads[pair, :, rows, :].reshape(2 * TOK, HEAD_SIZE)
+    grads = r.d_att_rows[block, :, pair * 128 : (pair + 1) * 128]
+    grads = jnp.concatenate([grads[:, :HEAD_SIZE], grads[:, HEAD_SIZE:]], axis=0)
+    keys_in, values_in = r.k_heads[pair, :keys, :], r.v_heads[pair, :keys, :]
+    scores = dot_nt(queries, keys_in).reshape(2, TOK, keys) * SCORE_SCALE
+    log_total = jnp.stack([r.log_total[rows, 2 * pair + g : 2 * pair + g + 1] for g in range(2)])
+    chances = jnp.exp(scores - log_total)
+    chances = jnp.where(allowed_block(r, block, keys)[None], chances, 0.0)
+    d_chances = dot_nt(grads, values_in).reshape(2, TOK, keys)
+    row_dots = jnp.sum(d_chances * chances, axis=-1, keepdims=True)
+    d_scores = (chances * (d_chances - row_dots)).astype(BF).reshape(2 * TOK, keys)
+    d_query = (dot(d_scores, keys_in) * SCORE_SCALE).astype(BF)
+    r.d_query[rows, pair * 128 : (pair + 1) * 128] = jnp.concatenate(
+        [d_query[:TOK], d_query[TOK:]], axis=-1
+    )
+    d_key = dot_tn(d_scores, queries) * SCORE_SCALE
+    d_value = dot_tn(chances.astype(BF).reshape(2 * TOK, keys), grads)
+    if block == ROW // TOK - 1:
+        r.d_kv[pair, :, :HEAD_SIZE] = d_key
+        r.d_kv[pair, :, HEAD_SIZE:] = d_value
+    else:
+        r.d_kv[pair, :keys, :HEAD_SIZE] += d_key
+        r.d_kv[pair, :keys, HEAD_SIZE:] += d_value
+
+
+def norm_back_unit(upstream, values):
+    inverse = lax.rsqrt(jnp.mean(values * values, axis=-1, keepdims=True) + EPS)
+    unit = values * inverse
+    d_values = inverse * (
+        upstream - unit * jnp.mean(upstream * unit, axis=-1, keepdims=True)
+    )
+    return d_values, jnp.sum(upstream * unit, axis=0, keepdims=True)
+
+
+def unit_norm(values):
+    return values * lax.rsqrt(jnp.mean(values * values, axis=-1, keepdims=True) + EPS)
+
+
+def own_parts(r):
+    scale = r.attn_gain[...]
+    for o in range(SEQ):
+        for ref, first, size in ((r.w_query, 0, OWN_Q), (r.w_key, OWN_Q, OWN_K), (r.w_value, OWN_Q + OWN_K, OWN_K)):
+            part = ref[:, o * size : (o + 1) * size].astype(F32) * scale
+            r.w_qkv[o, :, first : first + size] = part.astype(BF)
+
+
+def own_units(r):
+    scale = r.ffn_gain[...]
+    for ref, first in ((r.w_gate, 0), (r.w_up, FF_OWN)):
+        scaled = ref[...].astype(F32) * scale
+        for o in range(SEQ):
+            parts = [scaled[:, (4 * j + o) * FF_SHARD : (4 * j + o + 1) * FF_SHARD] for j in range(8)]
+            r.w_gu[o, :, first : first + FF_OWN] = jnp.concatenate(parts, axis=1).astype(BF)
+
+
+def rotation_tables(r, half):
+    size = ROW // 2
+    rows = pl.ds(half * size, size)
+    place = lax.broadcasted_iota(jnp.int32, (size, 1), 0) + half * size
+    begin = jnp.zeros((size, 1), jnp.int32)
+    for k in range(4):
+        start = r.doc_starts[0, k]
+        begin = jnp.maximum(begin, jnp.where(place >= start, start, 0))
+    angles = (place - begin).astype(F32) * r.frequency[...]
+    r.cosine[rows, :] = jnp.cos(angles)
+    r.sine[rows, :] = jnp.sin(angles)
+
+
+def head_forward(r):
+    first, low = lane_masks(TOK)
+
+    @pl.loop(0, SEQ)
+    def _(t):
+        rows = pl.ds(pl.multiple_of(t * TOK, TOK), TOK)
+        linear = dot(r.u_rows[t], r.qkv_all[...].reshape(WIDTH, QKV))
+        r.q_linear[rows, :] = linear[:, :OWN_Q]
+        r.k_linear[rows, :] = linear[:, OWN_Q : OWN_Q + OWN_K]
+        cosine, sine = r.cosine[rows, :], r.sine[rows, :]
+        for pair in range(2):
+            part = linear[:, pair * 128 : (pair + 1) * 128]
+            part = norm_rope(part, r.q_gain[...], cosine, sine, first, low).astype(BF)
+            r.q_heads[pair, 0, rows, :] = part[:, :HEAD_SIZE]
+            r.q_heads[pair, 1, rows, :] = part[:, HEAD_SIZE:]
+        part = linear[:, OWN_Q : OWN_Q + OWN_K]
+        part = norm_rope(part, r.k_gain[...], cosine, sine, first, low).astype(BF)
+        r.k_heads[0, rows, :] = part[:, :HEAD_SIZE]
+        r.k_heads[1, rows, :] = part[:, HEAD_SIZE:]
+        part = linear[:, OWN_Q + OWN_K :].astype(BF)
+        r.v_heads[0, rows, :] = part[:, :HEAD_SIZE]
+        r.v_heads[1, rows, :] = part[:, HEAD_SIZE:]
+
+
+def head_backward(r):
+    first, low = lane_masks(TOK)
+    r.head_gain_part[...] = jnp.zeros((2, 128), F32)
+
+    @pl.loop(0, SEQ)
+    def _(t):
+        rows = pl.ds(pl.multiple_of(t * TOK, TOK), TOK)
+        cosine, sine = r.cosine[rows, :], r.sine[rows, :]
+        for pair in range(2):
+            cols = slice(pair * 128, (pair + 1) * 128)
+            up = r.d_query[rows, cols].astype(F32)
+            back, gain_part = norm_rope_back(up, r.q_linear[rows, cols], r.q_gain[...], cosine, sine, first, low)
+            r.d_qkv[rows, cols] = back.astype(BF)
+            r.head_gain_part[0:1] += gain_part
+        up = jnp.concatenate([r.d_kv[0, rows, :HEAD_SIZE], r.d_kv[1, rows, :HEAD_SIZE]], axis=-1)
+        up = up.astype(BF).astype(F32)
+        back, gain_part = norm_rope_back(up, r.k_linear[rows, :], r.k_gain[...], cosine, sine, first, low)
+        r.d_qkv[rows, OWN_Q : OWN_Q + OWN_K] = back.astype(BF)
+        r.head_gain_part[1:2] += gain_part
+        up = jnp.concatenate([r.d_kv[0, rows, HEAD_SIZE:], r.d_kv[1, rows, HEAD_SIZE:]], axis=-1)
+        r.d_qkv[rows, OWN_Q + OWN_K :] = up.astype(BF)
+
+
+def units_up(r, t):
+    gate_up = dot(r.mid_rows[t], r.gu_all[...].reshape(WIDTH, HIDDEN_TWO))
+    gate, up = gate_up[:, :FF_OWN], gate_up[:, FF_OWN:]
+    sigmoid = 1.0 / (1.0 + jnp.exp(-gate))
+    swish = gate * sigmoid
+    r.active[t] = (swish * up).astype(BF)
+    blocks = pl.ds(8 * t, 8)
+    by_gate = up * (sigmoid * (1.0 + gate * (1.0 - sigmoid)))
+    r.d_gu[blocks, :, :FF_OWN] = by_gate.astype(BF).reshape(8, 32, FF_OWN)
+    r.d_gu[blocks, :, FF_OWN:] = swish.astype(BF).reshape(8, 32, FF_OWN)
+
+
+def units_down(r, t):
+    d_active = dot_nt(r.cot_rows[t], r.down_all[...].reshape(FF_OWN, WIDTH)).reshape(8, 32, FF_OWN)
+    blocks = pl.ds(8 * t, 8)
+    r.d_gu[blocks, :, :FF_OWN] = (d_active * r.d_gu[blocks, :, :FF_OWN].astype(F32)).astype(BF)
+    r.d_gu[blocks, :, FF_OWN:] = (d_active * r.d_gu[blocks, :, FF_OWN:].astype(F32)).astype(BF)
+    d_gu = r.d_gu[blocks].reshape(TOK, HIDDEN_TWO)
+    return dot_nt(d_gu, r.gu_all[...].reshape(WIDTH, HIDDEN_TWO))
+
+
+def whole_block(r):
+    l = r.links = Links(r.send_sems, r.recv_sems)
+    l.greet(pltpu.get_barrier_semaphore(), l.everyone())
+    x = r.inputs[...].astype(F32)
+    r.u_rows[l.s] = unit_norm(x).astype(BF)
+    own_parts(r)
+    own_units(r)
+    r.out_all[l.dp, l.s] = r.w_out[...]
+    r.qkv_all[l.dp, l.s] = r.w_qkv[l.s]
+    r.gu_all[l.dp, l.s] = r.w_gu[l.s]
+    r.down_all[l.dp] = r.w_down[...]
+    r.cot_rows[l.s] = r.cotangent[...]
+    pl.semaphore_wait(pltpu.get_barrier_semaphore(), len(l.everyone()))
+    qkv_cols = [l.push(r.w_qkv.at[o], r.qkv_all.at[l.dp, l.s], s=o) for o in l.others]
+    out = Gather(l, lambda b: r.out_all.at[b, l.s])
+    qkv = Gather(l, lambda b: r.qkv_all.at[b])
+    gate_up = [Gather(l, lambda b, g=g: r.gu_all.at[b, g]) for g in (l.s,) + l.others]
+    down_a = Gather(l, lambda b: r.down_all.at[b, pl.ds(0, DOWN_A)])
+    down_b = PairGather(l, lambda b: r.down_all.at[b, pl.ds(DOWN_A, DOWN_B)])
+    out.start_z()
+    out.start_y()
+    gu_cols = [l.push(r.w_gu.at[o], r.gu_all.at[l.dp, l.s], s=o) for o in l.others]
+    u_far = l.push(r.u_rows.at[l.s], r.u_rows.at[l.s], s=l.s2)
+    u_near = l.push(r.u_rows.at[l.s], r.u_rows.at[l.s], s=l.s1)
+    for copy in qkv_cols:
+        copy.wait_recv()
+    qkv.start_z()
+    qkv.start_y()
+    down_a.start_y()
+    down_b.start_y()
+    gate_up[0].start_y()
+    out.step(0)
+    qkv.step(0)
+    rotation_tables(r, 0)
+    out.step(1)
+    qkv.step(1)
+    rotation_tables(r, 1)
+    out.step(2)
+    qkv.step(2)
+    gate_up[0].start_z()
+    for k in range(3):
+        gu_cols[k].wait_recv()
+        gate_up[1 + k].start_z()
+        gate_up[1 + k].start_y()
+    u_far.wait_recv()
+    u_more = l.push(r.u_rows.at[l.s2], r.u_rows.at[l.s2], s=l.s1)
+    out.finish()
+    out_far = l.push(r.out_all.at[:, l.s], r.out_all.at[:, l.s], s=l.s2)
+    out_near = l.push(r.out_all.at[:, l.s], r.out_all.at[:, l.s], s=l.s1)
+    qkv.finish()
+    u_near.wait_recv()
+    u_more.wait_recv()
+    for piece in gate_up[:2]:
+        piece.step(0)
+    head_forward(r)
+    for piece in gate_up[2:]:
+        piece.step(0)
+    attention_block(r, 0, 3)
+    attention_block(r, 1, 3)
+    gate_up[0].step(1)
+    attention_block(r, 0, 2)
+    attention_block(r, 1, 2)
+    gate_up[1].step(1)
+    out_far.wait_recv()
+    out_more = l.push(r.out_all.at[:, l.s2], r.out_all.at[:, l.s2], s=l.s1)
+    attention_block(r, 0, 1)
+    attention_block(r, 1, 1)
+    gate_up[2].step(1)
+    attention_block(r, 0, 0)
+    attention_block(r, 1, 0)
+    att = [l.push(r.att_own.at[o], r.att_local.at[l.s], s=o) for o in l.others]
+    cot_far = l.push(r.cot_rows.at[l.s], r.cot_rows.at[l.s], s=l.s2)
+    cot_near = l.push(r.cot_rows.at[l.s], r.cot_rows.at[l.s], s=l.s1)
+    r.att_local[l.s] = r.att_own[l.s]
+    gate_up[3].step(1)
+    down_a.start_z()
+    gate_up[0].step(2)
+    out_near.wait_recv()
+    out_more.wait_recv()
+    for copy in att:
+        copy.wait_recv()
+    middle = x
+    for part in range(SEQ):
+        rows = r.out_all[part * 2 : (part + 1) * 2].reshape(OWN_Q, WIDTH)
+        middle = middle + dot(r.att_local[part], rows)
+    r.middle[...] = middle
+    r.mid_rows[l.s] = unit_norm(middle).astype(BF)
+    mid_far = l.push(r.mid_rows.at[l.s], r.mid_rows.at[l.s], s=l.s2)
+    mid_near = l.push(r.mid_rows.at[l.s], r.mid_rows.at[l.s], s=l.s1)
+    for piece in gate_up[1:]:
+        piece.step(2)
+    down_a.step(0)
+    down_b.start_z()
+    cot_far.wait_recv()
+    cot_more = l.push(r.cot_rows.at[l.s2], r.cot_rows.at[l.s2], s=l.s1)
+    down_b.join()
+    mid_far.wait_recv()
+    mid_more = l.push(r.mid_rows.at[l.s2], r.mid_rows.at[l.s2], s=l.s1)
+    down_a.step(1)
+    down_b.step(0)
+    down_a.step(2)
+    mid_near.wait_recv()
+    mid_more.wait_recv()
+    for piece in gate_up:
+        piece.finish()
+    units_up(r, l.s3)
+    units_up(r, l.s2)
+    down_b.step(1)
+    units_up(r, l.s1)
+    units_up(r, l.s)
+    down_b.step(2)
+    cot_near.wait_recv()
+    cot_more.wait_recv()
+    for t in range(SEQ):
+        r.flipped[:, t * TOK : (t + 1) * TOK] = r.active[t].T
+    cot = r.cot_rows[...].reshape(ROW, WIDTH)
+
+    @pl.loop(0, 4)
+    def _(k):
+        rows = pl.ds(pl.multiple_of(k * 288, 32), 288)
+        grad = dot(r.flipped[rows, :], cot).astype(BF)
+        r.down_part[pl.ds(2 * k, 2)] = grad.reshape(2, FF_SHARD, WIDTH)
+
+    down_a_sum = Scatter(
+        l, lambda b: r.down_part.at[b, pl.ds(0, DOWN_A)], lambda k: r.down_a_slots.at[k], lambda k: r.down_a_slots.at[4 + k]
+    )
+    down_b_sum = PairScatter(
+        l,
+        lambda b: r.down_part.at[b, pl.ds(DOWN_A, DOWN_B)],
+        r.down_b_slots.at[10],
+        lambda k: r.down_b_slots.at[k],
+        lambda k: r.down_b_slots.at[5 + k],
+    )
+    down_a_sum.start()
+    down_b_sum.start()
+    down_b_sum.step(0)
+    down_a.finish()
+    d_mid = RowSum(l, r.slots_a)
+    r.parts[0] = units_down(r, l.s3).astype(BF).reshape(8, 32, WIDTH)
+    d_mid.hand_over(r.parts.at[0])
+    r.parts[1] = units_down(r, l.s2).astype(BF).reshape(8, 32, WIDTH)
+    d_mid.cross(r.parts.at[1])
+    down_b_sum.step(1)
+    r.parts[2] = units_down(r, l.s1).astype(BF).reshape(8, 32, WIDTH)
+    d_mid.near(r.parts.at[2])
+    own = units_down(r, l.s)
+    down_b_sum.step(2)
+    d_values, ffn_gain_part = norm_back_unit(d_mid.total(own), r.middle[...])
+    d_middle = r.cotangent[...].astype(F32) + d_values
+    r.input_grad[...] = d_middle
+    d_branch = d_middle.astype(BF)
+    r.gains[0, 1:2, :] = ffn_gain_part
+    l.drain()
+    for part in range(SEQ):
+        rows = r.out_all[part * 2 : (part + 1) * 2].reshape(OWN_Q, WIDTH)
+        r.att_own[part] = dot_nt(d_branch, rows).astype(BF)
+    d_att = [l.push(r.att_own.at[o], r.d_att_rows.at[l.s], s=o) for o in l.others]
+    r.d_att_rows[l.s] = r.att_own[l.s]
+    for part in range(SEQ):
+        grad = dot_tn(r.att_local[part], d_branch).astype(BF)
+        r.out_all[2 * part : 2 * part + 2] = grad.reshape(2, 4, 32, WIDTH)
+    for t in range(SEQ):
+        r.flipped[:WIDTH, t * TOK : (t + 1) * TOK] = r.mid_rows[t].T
+    d_gu = r.d_gu[0:32].reshape(ROW, HIDDEN_TWO)
+
+    @pl.loop(0, 4)
+    def _(k):
+        rows = pl.ds(pl.multiple_of(k * 256, 256), 256)
+        grad = dot(r.flipped[rows, :], d_gu).astype(BF)
+        r.gu_all[pl.ds(2 * k, 2)] = grad.reshape(2, 4, 32, HIDDEN_TWO)
+
+    l.greet(r.free, l.column())
+    pl.semaphore_wait(r.free, len(l.column()))
+    gu_sums = [
+        Scatter(
+            l,
+            lambda b, g=g: r.gu_all.at[b, g],
+            lambda k, n=n: r.d_gu.at[4 * n + k],
+            lambda k, n=n: r.d_gu.at[16 + 5 * n + k],
+        )
+        for n, g in enumerate(l.others + (l.s,))
+    ]
+    for piece in gu_sums:
+        piece.start()
+    down_a_sum.join()
+    down_a_sum.step(0)
+    down_b_sum.cross()
+    for copy in d_att:
+        copy.wait_recv()
+    out_row = RowSum(l, r.slots_b)
+    out_row.hand_over(r.out_all.at[:, l.s3])
+    attention_block_back(r, 0, 3)
+    out_row.cross(r.out_all.at[:, l.s2])
+    out_row.near(r.out_all.at[:, l.s1])
+    down_a_sum.step(1)
+    attention_block_back(r, 1, 3)
+    attention_block_back(r, 0, 2)
+    down_a_sum.step(2)
+    attention_block_back(r, 1, 2)
+    gu_sums[0].join()
+    gu_sums[0].step(0)
+    attention_block_back(r, 0, 1)
+    attention_block_back(r, 1, 1)
+    gu_sums[0].step(1)
+    attention_block_back(r, 0, 0)
+    attention_block_back(r, 1, 0)
+    gu_sums[0].step(2)
+    out_total = out_row.total(r.out_all[:, l.s].astype(F32))
+    r.out_all[:, l.s] = out_total.astype(BF)
+    head_backward(r)
+    d_u = RowSum(l, r.slots_a)
+    weights = r.qkv_all[...].reshape(WIDTH, QKV)
+
+    def d_u_part(t):
+        return dot_nt(r.d_qkv[pl.ds(pl.multiple_of(t * TOK, TOK), TOK), :], weights)
+
+    r.parts[0] = d_u_part(l.s3).astype(BF).reshape(8, 32, WIDTH)
+    d_u.hand_over(r.parts.at[0])
+    r.parts[1] = d_u_part(l.s2).astype(BF).reshape(8, 32, WIDTH)
+    d_u.cross(r.parts.at[1])
+    r.parts[2] = d_u_part(l.s1).astype(BF).reshape(8, 32, WIDTH)
+    d_u.near(r.parts.at[2])
+    own = d_u_part(l.s)
+    gu_sums[1].join()
+    gu_sums[1].step(0)
+    for t in range(SEQ):
+        r.flipped[:WIDTH, t * TOK : (t + 1) * TOK] = r.u_rows[t].T
+    grad = dot(r.flipped[:WIDTH, :], r.d_qkv[...]).astype(BF)
+    r.qkv_all[...] = grad.reshape(8, 4, 32, QKV)
+    qkv_sum = Scatter(l, lambda b: r.qkv_all.at[b], lambda k: r.qkv_slots.at[k], lambda k: r.qkv_slots.at[4 + k])
+    qkv_sum.start()
+    out_sum = Scatter(
+        l, lambda b: r.out_all.at[b, l.s], lambda k: r.out_slots.at[k], lambda k: r.out_slots.at[4 + k]
+    )
+    out_sum.start()
+    gu_sums[1].step(1)
+    x = r.inputs[...].astype(F32)
+    d_values, attn_gain_part = norm_back_unit(d_u.total(own), x)
+    r.input_grad[...] += d_values
+    r.gains[0, 0:1, :] = attn_gain_part
+    r.gains[0, 2:3, 0:128] = r.head_gain_part[0:1]
+    r.gains[0, 2:3, 128:256] = r.head_gain_part[1:2]
+    r.gains[0, 2:3, 256:] = jnp.zeros((1, WIDTH - 256), F32)
+    r.gains[0, 3:8, :] = jnp.zeros((5, WIDTH), F32)
+    gains = [l.push(r.gains.at[0], r.gain_slots.at[k], s=o) for k, o in enumerate(l.others)]
+    d_u.links.settle((d_u.first, d_u.second, d_u.third))
+    gu_sums[1].step(2)
+    down_all = r.down_all[...].reshape(FF_OWN, WIDTH)
+    last = RowSum(l, r.slots_b)
+    r.parts[0] = dot(r.active[l.s3], down_all).astype(BF).reshape(8, 32, WIDTH)
+    last.hand_over(r.parts.at[0])
+    r.parts[1] = dot(r.active[l.s2], down_all).astype(BF).reshape(8, 32, WIDTH)
+    last.cross(r.parts.at[1])
+    r.parts[2] = dot(r.active[l.s1], down_all).astype(BF).reshape(8, 32, WIDTH)
+    last.near(r.parts.at[2])
+    own = r.middle[...] + dot(r.active[l.s], down_all)
+    for copy in gains:
+        copy.wait_recv()
+    r.gains[1] = r.gains[0] + r.gain_slots[0] + r.gain_slots[1] + r.gain_slots[2]
+    gains_y = l.push(r.gains.at[1], r.gain_slots.at[3], dp=l.y_peer)
+    gu_sums[2].join()
+    gu_sums[2].step(0)
+    home = []
+    r.gu_sum[0] = gu_sums[0].total().astype(BF)
+    home.append(l.push(r.gu_sum.at[0], r.gu_grad.at[l.s], s=l.s1))
+    gu_sums[2].step(1)
+    r.down_grad[0:DOWN_A] = down_a_sum.total()
+    r.down_grad[DOWN_A:] = down_b_sum.total()
+    r.gu_sum[1] = gu_sums[1].total().astype(BF)
+    home.append(l.push(r.gu_sum.at[1], r.gu_grad.at[l.s], s=l.s2))
+    gu_sums[2].step(2)
+    r.output[...] = last.total(own).astype(BF)
+    gu_sums[3].join()
+    gu_sums[3].step(0)
+    gains_y.wait_recv()
+    r.gains[2] = r.gains[1] + r.gain_slots[3]
+    gains_z = [l.push(r.gains.at[2], r.gain_slots.at[4 + k], dp=p) for k, p in enumerate(l.z_peers)]
+    gu_sums[3].step(1)
+    r.gu_sum[2] = gu_sums[2].total().astype(BF)
+    home.append(l.push(r.gu_sum.at[2], r.gu_grad.at[l.s], s=l.s3))
+    gu_sums[3].step(2)
+    qkv_sum.join()
+    qkv_sum.step(0)
+    out_sum.join()
+    out_sum.step(0)
+    qkv_sum.step(1)
+    out_sum.step(1)
+    qkv_sum.step(2)
+    out_sum.step(2)
+    r.gu_grad[l.s] = gu_sums[3].total().astype(BF)
+    r.qkv_sum[...] = qkv_sum.total().astype(BF)
+    home += [l.push(r.qkv_sum.at[o], r.qkv_grad.at[l.s], s=o) for o in l.others]
+    r.qkv_grad[l.s] = r.qkv_sum[l.s]
+    r.out_grad[...] = out_sum.total()
+    for copy in gains_z + home:
+        copy.wait_recv()
+    r.gain_grads[...] = r.gains[2] + r.gain_slots[4] + r.gain_slots[5] + r.gain_slots[6]
+    l.drain()
+
+
+class Names:
+    pass
+
+
+def frequencies():
+    steps = np.arange(HEAD_SIZE // 2, dtype=np.float64) * (2.0 / HEAD_SIZE)
+    return jnp.asarray(np.tile(THETA ** (-steps), 4)[None], F32)
+
+
+MAX_COPIES = 260
+VMEM_BYTES = 63 * 2**20
+
+
+def on_device_in_kernels(
+    inputs,
+    doc_starts,
+    cotangent,
+    attn_gain,
+    w_query,
+    key_projection_weight,
+    value_projection_weight,
+    q_gain,
+    k_gain,
+    w_out,
+    ffn_gain,
+    w_gate,
+    w_up,
+    w_down,
+):
+    given = dict(
+        inputs=inputs,
+        cotangent=cotangent,
+        attn_gain=attn_gain.astype(F32)[:, None],
+        ffn_gain=ffn_gain.astype(F32)[:, None],
+        q_gain=jnp.tile(q_gain.astype(F32), 2)[None],
+        k_gain=jnp.tile(k_gain.astype(F32), 2)[None],
+        w_query=w_query,
+        w_key=key_projection_weight,
+        w_value=value_projection_weight,
+        w_out=w_out,
+        w_gate=w_gate,
+        w_up=w_up,
+        w_down=w_down,
+        frequency=frequencies(),
+        doc_starts=doc_starts,
+    )
+    results = dict(
+        output=((TOK, WIDTH), BF),
+        input_grad=((TOK, WIDTH), F32),
+        down_grad=((FF_SHARD, WIDTH), F32),
+        out_grad=((32, WIDTH), F32),
+        gu_grad=((SEQ, 32, HIDDEN_TWO), BF),
+        qkv_grad=((SEQ, 32, QKV), BF),
+        gain_grads=((8, WIDTH), F32),
+    )
+    kept = dict(
+        w_qkv=((SEQ, 32, QKV), BF),
+        w_gu=((SEQ, 32, HIDDEN_TWO), BF),
+        cosine=((ROW, 128), F32),
+        sine=((ROW, 128), F32),
+        u_rows=((SEQ, TOK, WIDTH), BF),
+        cot_rows=((SEQ, TOK, WIDTH), BF),
+        mid_rows=((SEQ, TOK, WIDTH), BF),
+        qkv_all=((8, 4, 32, QKV), BF),
+        gu_all=((8, 4, 32, HIDDEN_TWO), BF),
+        down_all=((8, FF_SHARD, WIDTH), BF),
+        out_all=((8, 4, 32, WIDTH), BF),
+        q_linear=((ROW, OWN_Q), F32),
+        k_linear=((ROW, OWN_K), F32),
+        q_heads=((2, 2, ROW, HEAD_SIZE), BF),
+        k_heads=((2, ROW, HEAD_SIZE), BF),
+        v_heads=((2, ROW, HEAD_SIZE), BF),
+        log_total=((ROW, 128), F32),
+        att_own=((SEQ, TOK, OWN_Q), BF),
+        att_local=((SEQ, TOK, OWN_Q), BF),
+        middle=((TOK, WIDTH), F32),
+        active=((SEQ, TOK, FF_OWN), BF),
+        d_gu=((36, 32, HIDDEN_TWO), BF),
+        parts=((3, 8, 32, WIDTH), BF),
+        slots_a=((3, 8, 32, WIDTH), BF),
+        slots_b=((3, 8, 32, WIDTH), BF),
+        d_att_rows=((SEQ, TOK, OWN_Q), BF),
+        flipped=((FF_OWN, ROW), BF),
+        down_part=((8, FF_SHARD, WIDTH), BF),
+        down_a_slots=((9, DOWN_A, WIDTH), BF),
+        down_b_slots=((11, DOWN_B, WIDTH), BF),
+        out_slots=((9, 32, WIDTH), BF),
+        qkv_slots=((9, 4, 32, QKV), BF),
+        d_query=((ROW, OWN_Q), BF),
+        d_kv=((2, ROW, 128), F32),
+        d_qkv=((ROW, QKV), BF),
+        head_gain_part=((2, 128), F32),
+        gains=((3, 8, WIDTH), F32),
+        gain_slots=((7, 8, WIDTH), F32),
+        gu_sum=((3, 32, HIDDEN_TWO), BF),
+        qkv_sum=((4, 32, QKV), BF),
+    )
+
+    def body(*refs):
+        r = Names()
+        names = [*given, *results, *kept]
+        for name, ref in zip(names, refs):
+            setattr(r, name, ref)
+        r.send_sems, r.recv_sems, r.free = refs[len(names) :]
+        whole_block(r)
+
+    done = pl.pallas_call(
+        body,
+        out_shape=[jax.ShapeDtypeStruct(*result) for result in results.values()],
+        in_specs=[
+            pl.BlockSpec(memory_space=pltpu.SMEM if a is doc_starts else pltpu.VMEM) for a in given.values()
+        ],
+        out_specs=[pl.BlockSpec(memory_space=pltpu.VMEM)] * len(results),
+        scratch_shapes=[pltpu.VMEM(*shape) for shape in kept.values()]
+        + [
+            pltpu.SemaphoreType.DMA((MAX_COPIES,)),
+            pltpu.SemaphoreType.DMA((MAX_COPIES,)),
+            pltpu.SemaphoreType.REGULAR,
+        ],
+        compiler_params=pltpu.CompilerParams(
+            collective_id=0, has_side_effects=True, vmem_limit_bytes=VMEM_BYTES
+        ),
+        cost_estimate=pl.CostEstimate(flops=30_000_000_000, bytes_accessed=10_000_000, transcendentals=0),
+    )(*given.values())
+    output, input_grad, down_grad, out_grad, gu_grad, qkv_grad, gains = done
+    rows = w_query.shape[0]
+    attn_scale = attn_gain.astype(F32)[:, None]
+    ffn_scale = ffn_gain.astype(F32)[:, None]
+
+    def whole_heads(part):
+        return part.astype(F32).transpose(1, 0, 2).reshape(rows, -1) * attn_scale
+
+    def whole_units(part):
+        part = part.astype(F32).reshape(SEQ, rows, 8, FF_SHARD).transpose(1, 2, 0, 3)
+        return part.reshape(rows, -1) * ffn_scale
+
+    place = (lax.axis_index("dp") * SEQ + lax.axis_index("seq")) * rows
+    attn_part = lax.dynamic_slice(gains[0], (place,), (rows,)) / attn_gain.astype(F32)
+    ffn_part = lax.dynamic_slice(gains[1], (place,), (rows,)) / ffn_gain.astype(F32)
+    return (
+        output,
+        input_grad,
+        attn_part,
+        whole_heads(qkv_grad[..., :OWN_Q]),
+        whole_heads(qkv_grad[..., OWN_Q : OWN_Q + OWN_K]),
+        whole_heads(qkv_grad[..., OWN_Q + OWN_K :]),
+        gains[2, 0:64] + gains[2, 64:128],
+        gains[2, 128:192] + gains[2, 192:256],
+        out_grad,
+        ffn_part,
+        whole_units(gu_grad[..., :FF_OWN]),
+        whole_units(gu_grad[..., FF_OWN:]),
+        down_grad,
+    )
+
+
 def solution(mesh):
+    in_kernels = (mesh.shape["dp"], mesh.shape["seq"]) == (8, 4)
     placed = (
         P(("dp", "seq"), None),
         P("dp", None),
@@ -379,7 +1352,7 @@
         P(("dp", "seq"), None),
     )
     return jax.shard_map(
-        on_device,
+        on_device_in_kernels if in_kernels else on_device,
         mesh=mesh,
         in_specs=placed,
         out_specs=(

time: 1520 us -> 260 us (0.17)
  waiting for transfers between devices: 1130 us -> 0 us
  Pallas kernels: 0 us -> 236 us
  matrix products: 128 us -> 0 us
  blocking collectives: 85.9 us -> 0 us
  other arithmetic: 66.3 us -> 5.56 us
  local copies, waits for them, and re-layouts: 53.8 us -> 13.5 us
  starting transfers between devices: 30.7 us -> 0 us
    reduce_scatter x3 -> x0, waiting for transfers between devices: 761 us -> none  [the longest x1 405 us: on_device(): lax.psum_scatter(jnp.concatenate([first_part, second_part], axis=1), ('dp...]
    all_gather x7 -> x0, waiting for transfers between devices: 329 us -> none  [the longest x1 75.6 us: on_device(): lax.all_gather(w_down, ('dp', 'seq'), axis=0, tiled=True)]
    pallas_call x0 -> x1, Pallas kernels: none -> 236 us  [on_device_in_kernels(): pl.pallas_call(body, out_shape=[jax.ShapeDtypeStruct(*result) for result...]
    dot_general x32 -> x0, matrix products: 128 us -> none  [the longest x1 17.3 us: on_device(): lax.dot_general(normed_mid, ffn_columns, CONTRACT_ROWS, preferred_element...]
    unnamed x2 -> x0, blocking collectives: 85.9 us -> none
    all_to_all x8 -> x0, waiting for transfers between devices: 33.9 us -> none  [the longest x1 8.77 us: on_device(): lax.all_to_all(d_attended, 'seq', split_axis=1, concat_axis=0, tiled=True)]
    concatenate x3 -> x0, other arithmetic: 32.6 us -> none  [the longest x1 29.7 us: on_device(): jnp.concatenate([first_part, second_part], axis=1)]
    all_to_all x8 -> x0, starting transfers between devices: 30 us -> none  [the longest x1 4.14 us: on_device(): lax.all_to_all(d_q_heads, 'seq', split_axis=0, concat_axis=1, tiled=True)]
  transfers between devices with their start and end apart: 18 -> 0, of which waited for: 16 -> 0; matrix products, arithmetic and copies ran while one was open for 9% -> 0% of each run, Pallas kernels for 0% -> 0%
where the time goes in v1:
time: 260 us; the launch traced here: 256 us
  Pallas kernels  236 us (91%)
  local copies, waits for them, and re-layouts  13.5 us (5%)
  other arithmetic  5.56 us (2%)
    pallas_call x1, Pallas kernels, on_device_in_kernels(): pl.pallas_call(body, out_shape=[jax.ShapeDtypeStruct(*result) for result...  236 us
    unnamed x24, local copies, waits for them, and re-layouts  5.48 us

profile of v1, /device:TPU:0, one launch (start us, length us, event | category | flops | bytes accessed | tf_op | source)
XLA Modules:
  0.0 256.2 jit_solution(13061358651852894050)
XLA Ops:
  0.7 0.0 copy-start.8
  0.7 0.6 copy-done.8
  1.3 0.6 broadcast_in_dim_tile.6.refs_4_
  1.9 0.1 copy-done.9
  2.0 0.6 broadcast_in_dim_tile.7.refs_5_
  2.6 0.1 copy-done.6
  2.6 0.7 copy-done.7
  3.3 0.7 copy.32.refs_2_
  4.0 0.7 copy.33.refs_3_
  4.7 236.3 %shard_map.246 = (bf16[256,1024]{1,0:T(8,128)(2,1)}, f32[256,1024]{1,0:T(8,128)}, f32[144,1024]{1,0:T(8,128)}, f32[32,1024]{1,0:T(8,128)}, bf16[4,32,2304]{2,1,0...) custom-call(bf16[256,1024]{1,0:T(8,128)(2,1)} %refs_0_.1, bf16[256,1024]{1,0:T(8,128)(2,1)} %refs_1_.1, ...), custom_call_target="tpu_custom_call" | custom-call | flops 30000001024 | bytes 10000000 | tf_op jit(solution)/shard_map/pallas_call | solution.py:1286
  241.0 1.3 add_bitcast_fusion
  242.3 0.8 fusion
  243.1 0.6 bitcast_divide_fusion
  243.7 0.9 convert_bitcast_fusion
  244.7 0.7 broadcast_multiply_fusion.2
  245.4 0.2 copy-done.4
  245.6 0.7 bitcast_multiply_fusion
  246.3 0.1 slice_convert_fusion
  246.4 0.7 reshape.102
  247.1 0.7 copy.38
  247.8 0.9 reshape.93
  248.7 0.7 reshape.100
  249.4 0.7 copy.37
  250.1 0.9 reshape.91
  251.0 0.0 copy-start.3
  251.0 1.2 broadcast_multiply_fusion
  252.2 0.8 copy.48
  253.0 0.6 copy-done
  253.6 1.0 copy.49
  254.6 0.0 copy-done.5
  254.6 0.7 copy.50
  255.2 0.8 copy.51
  (17 shorter events, 0.1 us)
Async XLA Ops:
  0.7 0.7 copy-start.8
  1.3 0.7 copy-start.9
  2.0 0.7 copy-start.6
  2.6 0.7 copy-start.7
  243.7 2.6 %copy-start.1 = (bf16[4,32,2304]{2,1,0:T(8,128)(2,1)S(1)}, bf16[4,32,2304]{2,1,0:T(8,128)(2,1)}, u32[]{:S(2)}) copy-start(bf16[4,32,2304]{2,1,0:T(8,128)(2,1)} %get-tuple-element.25) | copy-start | bytes 1769476
  244.7 0.9 copy-start.4
  251.0 1.2 copy-start.3
  252.2 1.4 copy-start
  253.6 1.0 copy-start.5
  253.6 1.7 copy-start.2

commit v2 on v1

--- a/solution.py
+++ b/solution.py
@@ -380,6 +380,8 @@
 HIDDEN_TWO = 2304
 DOWN_A = 64
 DOWN_B = 80
+SUM_A = 96
+SUM_B = 48
 
 
 def flip(value, bit):
@@ -793,7 +795,7 @@
         scaled = ref[...].astype(F32) * scale
         for o in range(SEQ):
             parts = [scaled[:, (4 * j + o) * FF_SHARD : (4 * j + o + 1) * FF_SHARD] for j in range(8)]
-            r.w_gu[o, :, first : first + FF_OWN] = jnp.concatenate(parts, axis=1).astype(BF)
+            r.d_gu[32 + o, :, first : first + FF_OWN] = jnp.concatenate(parts, axis=1).astype(BF)
 
 
 def rotation_tables(r, half):
@@ -886,7 +888,7 @@
     own_units(r)
     r.out_all[l.dp, l.s] = r.w_out[...]
     r.qkv_all[l.dp, l.s] = r.w_qkv[l.s]
-    r.gu_all[l.dp, l.s] = r.w_gu[l.s]
+    r.gu_all[l.dp, l.s] = r.d_gu[32 + l.s]
     r.down_all[l.dp] = r.w_down[...]
     r.cot_rows[l.s] = r.cotangent[...]
     pl.semaphore_wait(pltpu.get_barrier_semaphore(), len(l.everyone()))
@@ -898,29 +900,32 @@
     down_b = PairGather(l, lambda b: r.down_all.at[b, pl.ds(DOWN_A, DOWN_B)])
     out.start_z()
     out.start_y()
-    gu_cols = [l.push(r.w_gu.at[o], r.gu_all.at[l.dp, l.s], s=o) for o in l.others]
+    gu_cols = [l.push(r.d_gu.at[32 + o], r.gu_all.at[l.dp, l.s], s=o) for o in l.others]
     u_far = l.push(r.u_rows.at[l.s], r.u_rows.at[l.s], s=l.s2)
     u_near = l.push(r.u_rows.at[l.s], r.u_rows.at[l.s], s=l.s1)
     for copy in qkv_cols:
         copy.wait_recv()
     qkv.start_z()
     qkv.start_y()
+    gate_up[0].start_z()
     down_a.start_y()
     down_b.start_y()
-    gate_up[0].start_y()
     out.step(0)
     qkv.step(0)
+    gu_cols[0].wait_recv()
+    gate_up[1].start_z()
     rotation_tables(r, 0)
     out.step(1)
     qkv.step(1)
+    gu_cols[1].wait_recv()
+    gate_up[2].start_z()
     rotation_tables(r, 1)
     out.step(2)
     qkv.step(2)
-    gate_up[0].start_z()
-    for k in range(3):
-        gu_cols[k].wait_recv()
-        gate_up[1 + k].start_z()
-        gate_up[1 + k].start_y()
+    gu_cols[2].wait_recv()
+    gate_up[3].start_z()
+    for piece in gate_up:
+        piece.start_y()
     u_far.wait_recv()
     u_more = l.push(r.u_rows.at[l.s2], r.u_rows.at[l.s2], s=l.s1)
     out.finish()
@@ -1000,21 +1005,23 @@
         grad = dot(r.flipped[rows, :], cot).astype(BF)
         r.down_part[pl.ds(2 * k, 2)] = grad.reshape(2, FF_SHARD, WIDTH)
 
+    down_a.finish()
+    l.drain()
     down_a_sum = Scatter(
-        l, lambda b: r.down_part.at[b, pl.ds(0, DOWN_A)], lambda k: r.down_a_slots.at[k], lambda k: r.down_a_slots.at[4 + k]
+        l, lambda b: r.down_part.at[b, pl.ds(0, SUM_A)], lambda k: r.down_a_slots.at[k], lambda k: r.down_a_slots.at[4 + k]
     )
     down_b_sum = PairScatter(
         l,
-        lambda b: r.down_part.at[b, pl.ds(DOWN_A, DOWN_B)],
+        lambda b: r.down_part.at[b, pl.ds(SUM_A, SUM_B)],
         r.down_b_slots.at[10],
         lambda k: r.down_b_slots.at[k],
         lambda k: r.down_b_slots.at[5 + k],
     )
+    d_mid = RowSum(l, r.slots_a)
+    home = []
     down_a_sum.start()
     down_b_sum.start()
     down_b_sum.step(0)
-    down_a.finish()
-    d_mid = RowSum(l, r.slots_a)
     r.parts[0] = units_down(r, l.s3).astype(BF).reshape(8, 32, WIDTH)
     d_mid.hand_over(r.parts.at[0])
     r.parts[1] = units_down(r, l.s2).astype(BF).reshape(8, 32, WIDTH)
@@ -1022,22 +1029,7 @@
     down_b_sum.step(1)
     r.parts[2] = units_down(r, l.s1).astype(BF).reshape(8, 32, WIDTH)
     d_mid.near(r.parts.at[2])
-    own = units_down(r, l.s)
-    down_b_sum.step(2)
-    d_values, ffn_gain_part = norm_back_unit(d_mid.total(own), r.middle[...])
-    d_middle = r.cotangent[...].astype(F32) + d_values
-    r.input_grad[...] = d_middle
-    d_branch = d_middle.astype(BF)
-    r.gains[0, 1:2, :] = ffn_gain_part
-    l.drain()
-    for part in range(SEQ):
-        rows = r.out_all[part * 2 : (part + 1) * 2].reshape(OWN_Q, WIDTH)
-        r.att_own[part] = dot_nt(d_branch, rows).astype(BF)
-    d_att = [l.push(r.att_own.at[o], r.d_att_rows.at[l.s], s=o) for o in l.others]
-    r.d_att_rows[l.s] = r.att_own[l.s]
-    for part in range(SEQ):
-        grad = dot_tn(r.att_local[part], d_branch).astype(BF)
-        r.out_all[2 * part : 2 * part + 2] = grad.reshape(2, 4, 32, WIDTH)
+    r.input_grad[...] = units_down(r, l.s)
     for t in range(SEQ):
         r.flipped[:WIDTH, t * TOK : (t + 1) * TOK] = r.mid_rows[t].T
     d_gu = r.d_gu[0:32].reshape(ROW, HIDDEN_TWO)
@@ -1054,39 +1046,65 @@
         Scatter(
             l,
             lambda b, g=g: r.gu_all.at[b, g],
-            lambda k, n=n: r.d_gu.at[4 * n + k],
-            lambda k, n=n: r.d_gu.at[16 + 5 * n + k],
+            lambda k, n=n: r.d_gu.at[9 * n + k],
+            lambda k, n=n: r.d_gu.at[9 * n + 4 + k],
         )
-        for n, g in enumerate(l.others + (l.s,))
+        for n, g in enumerate(l.others)
     ]
-    for piece in gu_sums:
-        piece.start()
+    own_gu_sum = PairScatter(
+        l,
+        lambda b: r.gu_all.at[b, l.s],
+        r.d_gu.at[37],
+        lambda k: r.d_gu.at[27 + k],
+        lambda k: r.d_gu.at[32 + k],
+    )
+    own_gu_sum.start()
+    own_gu_sum.step(0)
+    gu_sums[1].start()
+    d_values, ffn_gain_part = norm_back_unit(d_mid.total(r.input_grad[...]), r.middle[...])
+    d_middle = r.cotangent[...].astype(F32) + d_values
+    r.input_grad[...] = d_middle
+    d_branch = d_middle.astype(BF)
+    r.gains[0, 1:2, :] = ffn_gain_part
+    for part in range(SEQ):
+        rows = r.out_all[part * 2 : (part + 1) * 2].reshape(OWN_Q, WIDTH)
+        r.att_own[part] = dot_nt(d_branch, rows).astype(BF)
+    d_att = [l.push(r.att_own.at[o], r.d_att_rows.at[l.s], s=o) for o in l.others]
+    r.d_att_rows[l.s] = r.att_own[l.s]
+    gu_sums[2].start()
     down_a_sum.join()
     down_a_sum.step(0)
-    down_b_sum.cross()
+    own_gu_sum.step(1)
     for copy in d_att:
         copy.wait_recv()
+    l.settle((d_mid.first, d_mid.second, d_mid.third))
+    attention_block_back(r, 0, 3)
+    for part in range(SEQ):
+        grad = dot_tn(r.att_local[part], d_branch).astype(BF)
+        r.out_all[2 * part : 2 * part + 2] = grad.reshape(2, 4, 32, WIDTH)
     out_row = RowSum(l, r.slots_b)
     out_row.hand_over(r.out_all.at[:, l.s3])
-    attention_block_back(r, 0, 3)
     out_row.cross(r.out_all.at[:, l.s2])
     out_row.near(r.out_all.at[:, l.s1])
-    down_a_sum.step(1)
+    gu_sums[0].start()
+    own_gu_sum.step(2)
     attention_block_back(r, 1, 3)
     attention_block_back(r, 0, 2)
-    down_a_sum.step(2)
     attention_block_back(r, 1, 2)
-    gu_sums[0].join()
-    gu_sums[0].step(0)
     attention_block_back(r, 0, 1)
     attention_block_back(r, 1, 1)
-    gu_sums[0].step(1)
     attention_block_back(r, 0, 0)
     attention_block_back(r, 1, 0)
-    gu_sums[0].step(2)
+    gu_sums[1].join()
+    gu_sums[1].step(0)
+    down_b_sum.step(2)
+    down_a_sum.step(1)
+    head_backward(r)
     out_total = out_row.total(r.out_all[:, l.s].astype(F32))
     r.out_all[:, l.s] = out_total.astype(BF)
-    head_backward(r)
+    out_sum = Scatter(
+        l, lambda b: r.out_all.at[b, l.s], lambda k: r.out_slots.at[k], lambda k: r.out_slots.at[4 + k]
+    )
     d_u = RowSum(l, r.slots_a)
     weights = r.qkv_all[...].reshape(WIDTH, QKV)
 
@@ -1100,19 +1118,25 @@
     r.parts[2] = d_u_part(l.s1).astype(BF).reshape(8, 32, WIDTH)
     d_u.near(r.parts.at[2])
     own = d_u_part(l.s)
-    gu_sums[1].join()
-    gu_sums[1].step(0)
+    down_b_sum.cross()
+    gu_sums[1].step(1)
+    down_a_sum.step(2)
     for t in range(SEQ):
         r.flipped[:WIDTH, t * TOK : (t + 1) * TOK] = r.u_rows[t].T
     grad = dot(r.flipped[:WIDTH, :], r.d_qkv[...]).astype(BF)
     r.qkv_all[...] = grad.reshape(8, 4, 32, QKV)
     qkv_sum = Scatter(l, lambda b: r.qkv_all.at[b], lambda k: r.qkv_slots.at[k], lambda k: r.qkv_slots.at[4 + k])
+    gu_sums[2].join()
+    gu_sums[2].step(0)
     qkv_sum.start()
-    out_sum = Scatter(
-        l, lambda b: r.out_all.at[b, l.s], lambda k: r.out_slots.at[k], lambda k: r.out_slots.at[4 + k]
-    )
     out_sum.start()
-    gu_sums[1].step(1)
+    gu_sums[1].step(2)
+    gu_sums[0].join()
+    gu_sums[0].step(0)
+    r.gu_all[l.dp, l.s2] = gu_sums[1].total().astype(BF)
+    home.append(l.push(r.gu_all.at[l.dp, l.s2], r.gu_grad.at[l.s], s=l.s2))
+    gu_sums[2].step(1)
+    own_gu_sum.cross()
     x = r.inputs[...].astype(F32)
     d_values, attn_gain_part = norm_back_unit(d_u.total(own), x)
     r.input_grad[...] += d_values
@@ -1122,14 +1146,15 @@
     r.gains[0, 2:3, 256:] = jnp.zeros((1, WIDTH - 256), F32)
     r.gains[0, 3:8, :] = jnp.zeros((5, WIDTH), F32)
     gains = [l.push(r.gains.at[0], r.gain_slots.at[k], s=o) for k, o in enumerate(l.others)]
-    d_u.links.settle((d_u.first, d_u.second, d_u.third))
-    gu_sums[1].step(2)
+    l.settle((d_u.first, d_u.second, d_u.third))
     down_all = r.down_all[...].reshape(FF_OWN, WIDTH)
     last = RowSum(l, r.slots_b)
     r.parts[0] = dot(r.active[l.s3], down_all).astype(BF).reshape(8, 32, WIDTH)
     last.hand_over(r.parts.at[0])
     r.parts[1] = dot(r.active[l.s2], down_all).astype(BF).reshape(8, 32, WIDTH)
     last.cross(r.parts.at[1])
+    gu_sums[2].step(2)
+    gu_sums[0].step(1)
     r.parts[2] = dot(r.active[l.s1], down_all).astype(BF).reshape(8, 32, WIDTH)
     last.near(r.parts.at[2])
     own = r.middle[...] + dot(r.active[l.s], down_all)
@@ -1137,39 +1162,29 @@
         copy.wait_recv()
     r.gains[1] = r.gains[0] + r.gain_slots[0] + r.gain_slots[1] + r.gain_slots[2]
     gains_y = l.push(r.gains.at[1], r.gain_slots.at[3], dp=l.y_peer)
-    gu_sums[2].join()
-    gu_sums[2].step(0)
-    home = []
-    r.gu_sum[0] = gu_sums[0].total().astype(BF)
-    home.append(l.push(r.gu_sum.at[0], r.gu_grad.at[l.s], s=l.s1))
-    gu_sums[2].step(1)
-    r.down_grad[0:DOWN_A] = down_a_sum.total()
-    r.down_grad[DOWN_A:] = down_b_sum.total()
-    r.gu_sum[1] = gu_sums[1].total().astype(BF)
-    home.append(l.push(r.gu_sum.at[1], r.gu_grad.at[l.s], s=l.s2))
-    gu_sums[2].step(2)
+    gu_sums[0].step(2)
+    qkv_sum.join()
+    qkv_sum.step(0)
+    r.gu_all[l.dp, l.s3] = gu_sums[2].total().astype(BF)
+    home.append(l.push(r.gu_all.at[l.dp, l.s3], r.gu_grad.at[l.s], s=l.s3))
+    r.down_grad[SUM_A:] = down_b_sum.total()
+    qkv_sum.step(1)
+    r.gu_all[l.dp, l.s1] = gu_sums[0].total().astype(BF)
+    home.append(l.push(r.gu_all.at[l.dp, l.s1], r.gu_grad.at[l.s], s=l.s1))
+    out_sum.join()
+    out_sum.step(0)
+    qkv_sum.step(2)
+    r.down_grad[0:SUM_A] = down_a_sum.total()
     r.output[...] = last.total(own).astype(BF)
-    gu_sums[3].join()
-    gu_sums[3].step(0)
     gains_y.wait_recv()
     r.gains[2] = r.gains[1] + r.gain_slots[3]
     gains_z = [l.push(r.gains.at[2], r.gain_slots.at[4 + k], dp=p) for k, p in enumerate(l.z_peers)]
-    gu_sums[3].step(1)
-    r.gu_sum[2] = gu_sums[2].total().astype(BF)
-    home.append(l.push(r.gu_sum.at[2], r.gu_grad.at[l.s], s=l.s3))
-    gu_sums[3].step(2)
-    qkv_sum.join()
-    qkv_sum.step(0)
-    out_sum.join()
-    out_sum.step(0)
-    qkv_sum.step(1)
     out_sum.step(1)
-    qkv_sum.step(2)
+    r.gu_grad[l.s] = own_gu_sum.total().astype(BF)
+    r.qkv_all[l.dp] = qkv_sum.total().astype(BF)
+    home += [l.push(r.qkv_all.at[l.dp, o], r.qkv_grad.at[l.s], s=o) for o in l.others]
+    r.qkv_grad[l.s] = r.qkv_all[l.dp, l.s]
     out_sum.step(2)
-    r.gu_grad[l.s] = gu_sums[3].total().astype(BF)
-    r.qkv_sum[...] = qkv_sum.total().astype(BF)
-    home += [l.push(r.qkv_sum.at[o], r.qkv_grad.at[l.s], s=o) for o in l.others]
-    r.qkv_grad[l.s] = r.qkv_sum[l.s]
     r.out_grad[...] = out_sum.total()
     for copy in gains_z + home:
         copy.wait_recv()
@@ -1177,6 +1192,46 @@
     l.drain()
 
 
+def own_lanes(row, size):
+    place = (lax.axis_index("dp") * SEQ + lax.axis_index("seq")) * size
+    return pltpu.roll(row, lax.rem(WIDTH - place, WIDTH), 1)[:, :size]
+
+
+def column(row):
+    n = row.shape[1]
+    same = lax.broadcasted_iota(jnp.int32, (n, n), 0) == lax.broadcasted_iota(jnp.int32, (n, n), 1)
+    return jnp.sum(jnp.where(same, row, 0.0), axis=1, keepdims=True)
+
+
+def lay_out(
+    output, input_grad, down_grad, out_grad, gu_grad, qkv_grad, gains, attn_gain, ffn_gain,
+    output_o, input_o, attn_o, query_o, key_o, value_o, q_gain_o, k_gain_o, out_o, ffn_o, gate_o, up_o, down_o, sems,
+):
+    pairs = ((output, output_o), (input_grad, input_o), (down_grad, down_o), (out_grad, out_o))
+    copies = [pltpu.make_async_copy(src, dst, sems.at[n]) for n, (src, dst) in enumerate(pairs)]
+    for copy in copies:
+        copy.start()
+    scale = attn_gain[...]
+    for o in range(SEQ):
+        for ref, first, size in ((query_o, 0, OWN_Q), (key_o, OWN_Q, OWN_K), (value_o, OWN_Q + OWN_K, OWN_K)):
+            ref[:, o * size : (o + 1) * size] = qkv_grad[o, :, first : first + size].astype(F32) * scale
+    scale = ffn_gain[...]
+    for ref, first in ((gate_o, 0), (up_o, FF_OWN)):
+        parts = []
+        for j in range(8):
+            for o in range(SEQ):
+                part = gu_grad[o, :, first + j * FF_SHARD : first + (j + 1) * FF_SHARD]
+                parts.append(part.astype(F32) * scale)
+        ref[...] = jnp.concatenate(parts, axis=1)
+    size = attn_o.shape[0]
+    attn_o[...] = (column(own_lanes(gains[0:1, :], size)) / attn_gain[...]).reshape(size)
+    ffn_o[...] = (column(own_lanes(gains[1:2, :], size)) / ffn_gain[...]).reshape(size)
+    q_gain_o[...] = (gains[2:3, 0:64] + gains[2:3, 64:128]).reshape(HEAD_SIZE)
+    k_gain_o[...] = (gains[2:3, 128:192] + gains[2:3, 192:256]).reshape(HEAD_SIZE)
+    for copy in copies:
+        copy.wait()
+
+
 class Names:
     pass
 
@@ -1186,7 +1241,7 @@
     return jnp.asarray(np.tile(THETA ** (-steps), 4)[None], F32)
 
 
-MAX_COPIES = 260
+MAX_COPIES = 300
 VMEM_BYTES = 63 * 2**20
 
 
@@ -1234,7 +1289,6 @@
     )
     kept = dict(
         w_qkv=((SEQ, 32, QKV), BF),
-        w_gu=((SEQ, 32, HIDDEN_TWO), BF),
         cosine=((ROW, 128), F32),
         sine=((ROW, 128), F32),
         u_rows=((SEQ, TOK, WIDTH), BF),
@@ -1254,15 +1308,15 @@
         att_local=((SEQ, TOK, OWN_Q), BF),
         middle=((TOK, WIDTH), F32),
         active=((SEQ, TOK, FF_OWN), BF),
-        d_gu=((36, 32, HIDDEN_TWO), BF),
+        d_gu=((38, 32, HIDDEN_TWO), BF),
         parts=((3, 8, 32, WIDTH), BF),
         slots_a=((3, 8, 32, WIDTH), BF),
         slots_b=((3, 8, 32, WIDTH), BF),
         d_att_rows=((SEQ, TOK, OWN_Q), BF),
         flipped=((FF_OWN, ROW), BF),
         down_part=((8, FF_SHARD, WIDTH), BF),
-        down_a_slots=((9, DOWN_A, WIDTH), BF),
-        down_b_slots=((11, DOWN_B, WIDTH), BF),
+        down_a_slots=((9, SUM_A, WIDTH), BF),
+        down_b_slots=((11, SUM_B, WIDTH), BF),
         out_slots=((9, 32, WIDTH), BF),
         qkv_slots=((9, 4, 32, QKV), BF),
         d_query=((ROW, OWN_Q), BF),
@@ -1271,8 +1325,6 @@
         head_gain_part=((2, 128), F32),
         gains=((3, 8, WIDTH), F32),
         gain_slots=((7, 8, WIDTH), F32),
-        gu_sum=((3, 32, HIDDEN_TWO), BF),
-        qkv_sum=((4, 32, QKV), BF),
     )
 
     def body(*refs):
@@ -1301,35 +1353,34 @@
         ),
         cost_estimate=pl.CostEstimate(flops=30_000_000_000, bytes_accessed=10_000_000, transcendentals=0),
     )(*given.values())
-    output, input_grad, down_grad, out_grad, gu_grad, qkv_grad, gains = done
     rows = w_query.shape[0]
-    attn_scale = attn_gain.astype(F32)[:, None]
-    ffn_scale = ffn_gain.astype(F32)[:, None]
-
-    def whole_heads(part):
-        return part.astype(F32).transpose(1, 0, 2).reshape(rows, -1) * attn_scale
-
-    def whole_units(part):
-        part = part.astype(F32).reshape(SEQ, rows, 8, FF_SHARD).transpose(1, 2, 0, 3)
-        return part.reshape(rows, -1) * ffn_scale
-
-    place = (lax.axis_index("dp") * SEQ + lax.axis_index("seq")) * rows
-    attn_part = lax.dynamic_slice(gains[0], (place,), (rows,)) / attn_gain.astype(F32)
-    ffn_part = lax.dynamic_slice(gains[1], (place,), (rows,)) / ffn_gain.astype(F32)
-    return (
-        output,
-        input_grad,
-        attn_part,
-        whole_heads(qkv_grad[..., :OWN_Q]),
-        whole_heads(qkv_grad[..., OWN_Q : OWN_Q + OWN_K]),
-        whole_heads(qkv_grad[..., OWN_Q + OWN_K :]),
-        gains[2, 0:64] + gains[2, 64:128],
-        gains[2, 128:192] + gains[2, 192:256],
-        out_grad,
-        ffn_part,
-        whole_units(gu_grad[..., :FF_OWN]),
-        whole_units(gu_grad[..., FF_OWN:]),
-        down_grad,
+    shapes = [
+        ((TOK, WIDTH), BF),
+        ((TOK, WIDTH), F32),
+        ((rows,), F32),
+        ((rows, SEQ * OWN_Q), F32),
+        ((rows, SEQ * OWN_K), F32),
+        ((rows, SEQ * OWN_K), F32),
+        ((HEAD_SIZE,), F32),
+        ((HEAD_SIZE,), F32),
+        ((rows, WIDTH), F32),
+        ((rows,), F32),
+        ((rows, FF), F32),
+        ((rows, FF), F32),
+        ((FF_SHARD, WIDTH), F32),
+    ]
+    return tuple(
+        pl.pallas_call(
+            lay_out,
+            out_shape=[jax.ShapeDtypeStruct(*shape) for shape in shapes],
+            in_specs=[pl.BlockSpec(memory_space=pl.ANY)] * 4 + [pl.BlockSpec(memory_space=pltpu.VMEM)] * 5,
+            out_specs=[
+                pl.BlockSpec(memory_space=pl.ANY if n in (0, 1, 8, 12) else pltpu.VMEM) for n in range(13)
+            ],
+            scratch_shapes=[pltpu.SemaphoreType.DMA((4,))],
+            compiler_params=pltpu.CompilerParams(vmem_limit_bytes=24 * 2**20),
+            cost_estimate=pl.CostEstimate(flops=1_000_000, bytes_accessed=10_000_000, transcendentals=0),
+        )(*done, given["attn_gain"], given["ffn_gain"])
     )
 
 

time: 260 us -> 231 us (0.89)
  Pallas kernels: 236 us -> 215 us
  other arithmetic: 5.56 us -> 0.67 us
  local copies, waits for them, and re-layouts: 13.5 us -> 10.2 us
    pallas_call x1, Pallas kernels: 236 us -> 212 us  [on_device_in_kernels(): pl.pallas_call(body, out_shape=[jax.ShapeDtypeStruct(*result) for result...]
    reshape x7 -> x0, local copies, waits for them, and re-layouts: 4.57 us -> none  [the longest x6 4.56 us: whole_units(): return part.reshape(rows, -1) * ffn_scale]
    pallas_call x0 -> x1, Pallas kernels: none -> 3.07 us  [on_device_in_kernels(): pl.pallas_call(lay_out, out_shape=[jax.ShapeDtypeStruct(*shape) for shape...]
    mul x3 -> x0, other arithmetic: 2.62 us -> none  [the longest x2 1.46 us: whole_heads(): return part.astype(F32).transpose(1, 0, 2).reshape(rows, -1) * attn_scale]
where the time goes in v2:
time: 231 us; the launch traced here: 227 us
  Pallas kernels  215 us (93%)
  local copies, waits for them, and re-layouts  10.2 us (4%)
    pallas_call x1, Pallas kernels, on_device_in_kernels(): pl.pallas_call(body, out_shape=[jax.ShapeDtypeStruct(*result) for result...  212 us
    unnamed x24, local copies, waits for them, and re-layouts  7.68 us

profile of v2, /device:TPU:0, one launch (start us, length us, event | category | flops | bytes accessed | tf_op | source)
XLA Modules:
  0.0 227.0 jit_solution(3461042201968489945)
XLA Ops:
  0.6 0.0 copy-start.9
  0.7 0.7 bitcast_convert_fusion.1
  1.3 0.0 copy-done.9
  1.3 0.0 copy-start.10
  1.3 0.6 copy-done.10
  2.0 0.0 copy-start.11
  2.0 0.6 broadcast_in_dim_tile.6.refs_4_
  2.6 0.1 copy-done.11
  2.6 0.6 broadcast_in_dim_tile.7.refs_5_
  3.2 0.7 copy.29.refs_3_.ffn_gain
  3.9 0.7 copy.28.refs_2_.attn_gain
  4.6 0.0 copy-start.6
  4.6 0.0 copy-start.7
  4.6 212.0 %shard_map.246 = (bf16[256,1024]{1,0:T(8,128)(2,1)}, f32[256,1024]{1,0:T(8,128)}, f32[144,1024]{1,0:T(8,128)}, f32[32,1024]{1,0:T(8,128)}, bf16[4,32,2304]{2,1,0...) custom-call(bf16[256,1024]{1,0:T(8,128)(2,1)} %refs_0_.1, bf16[256,1024]{1,0:T(8,128)(2,1)} %refs_1_.1, ...), custom_call_target="tpu_custom_call" | custom-call | flops 30000001024 | bytes 10000000 | tf_op jit(solution)/shard_map/pallas_call | solution.py:1338
  216.7 0.0 copy-done.6
  216.7 0.0 copy-done.7
  216.7 0.0 copy-start
  216.7 1.2 copy-done
  217.9 0.0 copy-start.1
  217.9 1.1 copy-done.1
  219.0 0.0 copy-start.2
  219.0 1.1 copy-done.2
  220.0 0.0 copy-start.3
  220.0 1.0 copy-done.3
  221.1 0.0 copy-start.4
  221.1 0.9 copy-done.4
  222.0 0.0 copy-start.5
  222.0 0.9 copy-done.5
  222.9 0.0 copy-start.8
  222.9 0.8 copy-done.8
  223.7 3.1 %shard_map.247 = (bf16[256,1024]{1,0:T(8,128)(2,1)}, f32[256,1024]{1,0:T(8,128)}, f32[32]{0:T(128)}, f32[32,1024]{1,0:T(8,128)}, f32[32,512]{1,0:T(8,128)}, /*in...) custom-call(bf16[256,1024]{1,0:T(8,128)(2,1)S(1)} %copy-done.3, ...), custom_call_target="tpu_custom_call" | custom-call | flops 1000000 | bytes 10000000 | tf_op jit(solution)/shard_map/pallas_call | solution.py:1373
  (3 shorter events, 0.0 us)
Async XLA Ops:
  0.6 0.7 copy-start.9
  1.3 0.7 copy-start.10
  2.0 0.7 copy-start.11
  4.6 212.1 %copy-start.6 = (f32[32,1]{1,0:T(8,128)S(1)}, f32[32,1]{1,0:T(8,128)}, u32[]{:S(2)}) copy-start(f32[32,1]{1,0:T(8,128)} %copy.29.refs_3_.ffn_gain) | copy-start | bytes 388
  4.6 212.1 %copy-start.7 = (f32[32,1]{1,0:T(8,128)S(1)}, f32[32,1]{1,0:T(8,128)}, u32[]{:S(2)}) copy-start(f32[32,1]{1,0:T(8,128)} %copy.28.refs_2_.attn_gain) | copy-start | bytes 388
  216.7 1.2 copy-start
  217.9 1.1 copy-start.1
  219.0 1.1 copy-start.2
  220.0 1.0 copy-start.3
  221.1 0.9 copy-start.4
  222.0 0.9 copy-start.5
  222.9 0.8 copy-start.8

commit v3 on v2

--- a/solution.py
+++ b/solution.py
@@ -378,10 +378,10 @@
 FF_OWN = 1152
 FF_SHARD = 144
 HIDDEN_TWO = 2304
-DOWN_A = 64
-DOWN_B = 80
-SUM_A = 96
-SUM_B = 48
+DOWN_A = 80
+DOWN_B = 64
+SUM_A = 80
+SUM_B = 64
 
 
 def flip(value, bit):
@@ -405,6 +405,7 @@
         self.send_sems, self.recv_sems = send_sems, recv_sems
         self.used = 0
         self.open = []
+        self.late = []
         self.dp = lax.axis_index("dp")
         self.s = lax.axis_index("seq")
         self.s1 = flip(self.s, 1)
@@ -441,19 +442,23 @@
         )
         return copy
 
-    def push(self, src, dst, dp=None, s=None, when=None):
+    def push(self, src, dst, dp=None, s=None, when=None, late=False):
         copy = self.plan(src, dst, dp, s)
         if when is None:
             copy.start()
         else:
             pl.when(when)(copy.start)
-        self.open.append((copy, when))
+        (self.late if late else self.open).append((copy, when))
         return copy
 
     def settle(self, copies):
         for copy in copies:
             copy.wait_send()
         self.open = [item for item in self.open if all(item[0] is not copy for copy in copies)]
+
+    def drain_late(self):
+        self.open, self.late = self.late, []
+        self.drain()
 
     def drain(self):
         for copy, when in self.open:
@@ -584,9 +589,9 @@
 
         for d in range(PLANES):
             if d > j:
-                self.links.open.append((self.up[d], self.links.z == j))
+                self.links.late.append((self.up[d], self.links.z == j))
             if d < last - j:
-                self.links.open.append((self.down[d], self.links.z == last - j))
+                self.links.late.append((self.down[d], self.links.z == last - j))
 
     def total(self):
         l = self.links
@@ -610,7 +615,7 @@
         l = self.links
         self.order = [jnp.where(l.z < PLANES // 2, PLANES - 1 - k, k) for k in range(PLANES)]
         self.over_y = [
-            l.push(self.view(2 * d + 1 - l.y), self.y_slots(k), dp=l.y_peer) for k, d in enumerate(self.order)
+            l.push(self.view(2 * d + 1 - l.y), self.y_slots(k), dp=l.y_peer, late=True) for k, d in enumerate(self.order)
         ]
         self.chain.start()
 
@@ -645,7 +650,7 @@
         l = self.links
         block = self.view(2 * l.z + 1 - l.y)
         block[...] = self.far.total().astype(BF)
-        self.over_y = l.push(block, self.y_slot, dp=l.y_peer)
+        self.over_y = l.push(block, self.y_slot, dp=l.y_peer, late=True)
 
     def total(self):
         own = self.near.total()
@@ -781,8 +786,23 @@
     return values * lax.rsqrt(jnp.mean(values * values, axis=-1, keepdims=True) + EPS)
 
 
+def as_row(vector):
+    return vector[...].astype(F32).reshape(1, vector.shape[0])
+
+
+def twice(vector):
+    row = as_row(vector)
+    return jnp.concatenate([row, row], axis=1)
+
+
+def column(row):
+    n = row.shape[1]
+    same = lax.broadcasted_iota(jnp.int32, (n, n), 0) == lax.broadcasted_iota(jnp.int32, (n, n), 1)
+    return jnp.sum(jnp.where(same, row, 0.0), axis=1, keepdims=True)
+
+
 def own_parts(r):
-    scale = r.attn_gain[...]
+    scale = column(as_row(r.attn_gain))
     for o in range(SEQ):
         for ref, first, size in ((r.w_query, 0, OWN_Q), (r.w_key, OWN_Q, OWN_K), (r.w_value, OWN_Q + OWN_K, OWN_K)):
             part = ref[:, o * size : (o + 1) * size].astype(F32) * scale
@@ -790,7 +810,7 @@
 
 
 def own_units(r):
-    scale = r.ffn_gain[...]
+    scale = column(as_row(r.ffn_gain))
     for ref, first in ((r.w_gate, 0), (r.w_up, FF_OWN)):
         scaled = ref[...].astype(F32) * scale
         for o in range(SEQ):
@@ -823,11 +843,11 @@
         cosine, sine = r.cosine[rows, :], r.sine[rows, :]
         for pair in range(2):
             part = linear[:, pair * 128 : (pair + 1) * 128]
-            part = norm_rope(part, r.q_gain[...], cosine, sine, first, low).astype(BF)
+            part = norm_rope(part, twice(r.q_gain), cosine, sine, first, low).astype(BF)
             r.q_heads[pair, 0, rows, :] = part[:, :HEAD_SIZE]
             r.q_heads[pair, 1, rows, :] = part[:, HEAD_SIZE:]
         part = linear[:, OWN_Q : OWN_Q + OWN_K]
-        part = norm_rope(part, r.k_gain[...], cosine, sine, first, low).astype(BF)
+        part = norm_rope(part, twice(r.k_gain), cosine, sine, first, low).astype(BF)
         r.k_heads[0, rows, :] = part[:, :HEAD_SIZE]
         r.k_heads[1, rows, :] = part[:, HEAD_SIZE:]
         part = linear[:, OWN_Q + OWN_K :].astype(BF)
@@ -846,12 +866,12 @@
         for pair in range(2):
             cols = slice(pair * 128, (pair + 1) * 128)
             up = r.d_query[rows, cols].astype(F32)
-            back, gain_part = norm_rope_back(up, r.q_linear[rows, cols], r.q_gain[...], cosine, sine, first, low)
+            back, gain_part = norm_rope_back(up, r.q_linear[rows, cols], twice(r.q_gain), cosine, sine, first, low)
             r.d_qkv[rows, cols] = back.astype(BF)
             r.head_gain_part[0:1] += gain_part
         up = jnp.concatenate([r.d_kv[0, rows, :HEAD_SIZE], r.d_kv[1, rows, :HEAD_SIZE]], axis=-1)
         up = up.astype(BF).astype(F32)
-        back, gain_part = norm_rope_back(up, r.k_linear[rows, :], r.k_gain[...], cosine, sine, first, low)
+        back, gain_part = norm_rope_back(up, r.k_linear[rows, :], twice(r.k_gain), cosine, sine, first, low)
         r.d_qkv[rows, OWN_Q : OWN_Q + OWN_K] = back.astype(BF)
         r.head_gain_part[1:2] += gain_part
         up = jnp.concatenate([r.d_kv[0, rows, HEAD_SIZE:], r.d_kv[1, rows, HEAD_SIZE:]], axis=-1)
@@ -892,73 +912,71 @@
     r.down_all[l.dp] = r.w_down[...]
     r.cot_rows[l.s] = r.cotangent[...]
     pl.semaphore_wait(pltpu.get_barrier_semaphore(), len(l.everyone()))
-    qkv_cols = [l.push(r.w_qkv.at[o], r.qkv_all.at[l.dp, l.s], s=o) for o in l.others]
-    out = Gather(l, lambda b: r.out_all.at[b, l.s])
+    out = PairGather(l, lambda b: r.out_all.at[b, l.s])
     qkv = Gather(l, lambda b: r.qkv_all.at[b])
     gate_up = [Gather(l, lambda b, g=g: r.gu_all.at[b, g]) for g in (l.s,) + l.others]
     down_a = Gather(l, lambda b: r.down_all.at[b, pl.ds(0, DOWN_A)])
     down_b = PairGather(l, lambda b: r.down_all.at[b, pl.ds(DOWN_A, DOWN_B)])
-    out.start_z()
-    out.start_y()
-    gu_cols = [l.push(r.d_gu.at[32 + o], r.gu_all.at[l.dp, l.s], s=o) for o in l.others]
-    u_far = l.push(r.u_rows.at[l.s], r.u_rows.at[l.s], s=l.s2)
-    u_near = l.push(r.u_rows.at[l.s], r.u_rows.at[l.s], s=l.s1)
+    qkv_cols = [l.push(r.w_qkv.at[o], r.qkv_all.at[l.dp, l.s], s=o) for o in l.others]
+    gate_up[0].start_z()
+    gate_up[0].start_y()
     for copy in qkv_cols:
         copy.wait_recv()
     qkv.start_z()
+    out.start_y()
+    gu_cols = [l.push(r.d_gu.at[32 + o], r.gu_all.at[l.dp, l.s], s=o) for o in l.others]
+    out.start_z()
+    rotation_tables(r, 0)
+    down_b.start_y()
     qkv.start_y()
-    gate_up[0].start_z()
-    down_a.start_y()
-    down_b.start_y()
+    out.join()
+    u_far = l.push(r.u_rows.at[l.s], r.u_rows.at[l.s], s=l.s2)
+    u_near = l.push(r.u_rows.at[l.s], r.u_rows.at[l.s], s=l.s1)
+    qkv.step(0)
+    gu_cols[1].wait_recv()
+    gu_cols[2].wait_recv()
+    gu_cols[0].wait_recv()
     out.step(0)
-    qkv.step(0)
-    gu_cols[0].wait_recv()
+    gate_up[2].start_y()
+    rotation_tables(r, 1)
+    out.step(1)
+    gate_up[1].start_y()
+    qkv.step(1)
     gate_up[1].start_z()
-    rotation_tables(r, 0)
-    out.step(1)
-    qkv.step(1)
-    gu_cols[1].wait_recv()
-    gate_up[2].start_z()
-    rotation_tables(r, 1)
-    out.step(2)
-    qkv.step(2)
-    gu_cols[2].wait_recv()
-    gate_up[3].start_z()
-    for piece in gate_up:
-        piece.start_y()
     u_far.wait_recv()
     u_more = l.push(r.u_rows.at[l.s2], r.u_rows.at[l.s2], s=l.s1)
-    out.finish()
+    out.step(2)
+    gate_up[3].start_z()
+    qkv.step(2)
+    gate_up[0].step(0)
+    gate_up[3].step(0)
+    gate_up[3].start_y()
+    qkv.finish()
+    gate_up[1].step(0)
     out_far = l.push(r.out_all.at[:, l.s], r.out_all.at[:, l.s], s=l.s2)
     out_near = l.push(r.out_all.at[:, l.s], r.out_all.at[:, l.s], s=l.s1)
-    qkv.finish()
     u_near.wait_recv()
     u_more.wait_recv()
-    for piece in gate_up[:2]:
-        piece.step(0)
+    gate_up[0].step(1)
     head_forward(r)
-    for piece in gate_up[2:]:
-        piece.step(0)
+    down_a.start_z()
     attention_block(r, 0, 3)
     attention_block(r, 1, 3)
-    gate_up[0].step(1)
     attention_block(r, 0, 2)
     attention_block(r, 1, 2)
+    attention_block(r, 0, 1)
+    gate_up[0].step(2)
+    gate_up[3].step(1)
+    attention_block(r, 1, 1)
+    gate_up[2].start_z()
+    attention_block(r, 0, 0)
+    attention_block(r, 1, 0)
+    att = [l.push(r.att_own.at[o], r.att_local.at[l.s], s=o) for o in l.others]
+    r.att_local[l.s] = r.att_own[l.s]
+    gate_up[3].step(2)
     gate_up[1].step(1)
     out_far.wait_recv()
     out_more = l.push(r.out_all.at[:, l.s2], r.out_all.at[:, l.s2], s=l.s1)
-    attention_block(r, 0, 1)
-    attention_block(r, 1, 1)
-    gate_up[2].step(1)
-    attention_block(r, 0, 0)
-    attention_block(r, 1, 0)
-    att = [l.push(r.att_own.at[o], r.att_local.at[l.s], s=o) for o in l.others]
-    cot_far = l.push(r.cot_rows.at[l.s], r.cot_rows.at[l.s], s=l.s2)
-    cot_near = l.push(r.cot_rows.at[l.s], r.cot_rows.at[l.s], s=l.s1)
-    r.att_local[l.s] = r.att_own[l.s]
-    gate_up[3].step(1)
-    down_a.start_z()
-    gate_up[0].step(2)
     out_near.wait_recv()
     out_more.wait_recv()
     for copy in att:
@@ -971,28 +989,33 @@
     r.mid_rows[l.s] = unit_norm(middle).astype(BF)
     mid_far = l.push(r.mid_rows.at[l.s], r.mid_rows.at[l.s], s=l.s2)
     mid_near = l.push(r.mid_rows.at[l.s], r.mid_rows.at[l.s], s=l.s1)
-    for piece in gate_up[1:]:
-        piece.step(2)
+    down_b.start_z()
+    gate_up[1].step(2)
+    cot_far = l.push(r.cot_rows.at[l.s], r.cot_rows.at[l.s], s=l.s2)
+    cot_near = l.push(r.cot_rows.at[l.s], r.cot_rows.at[l.s], s=l.s1)
+    gate_up[2].step(0)
+    gate_up[2].step(1)
+    gate_up[2].step(2)
+    down_b.join()
+    down_a.start_y()
+    gate_up[1].finish()
+    gate_up[3].finish()
+    mid_far.wait_recv()
+    mid_more = l.push(r.mid_rows.at[l.s2], r.mid_rows.at[l.s2], s=l.s1)
+    mid_near.wait_recv()
+    mid_more.wait_recv()
     down_a.step(0)
-    down_b.start_z()
+    down_b.step(0)
+    gate_up[0].finish()
+    gate_up[2].finish()
+    units_up(r, l.s3)
+    down_a.step(1)
+    units_up(r, l.s2)
+    units_up(r, l.s1)
+    units_up(r, l.s)
     cot_far.wait_recv()
     cot_more = l.push(r.cot_rows.at[l.s2], r.cot_rows.at[l.s2], s=l.s1)
-    down_b.join()
-    mid_far.wait_recv()
-    mid_more = l.push(r.mid_rows.at[l.s2], r.mid_rows.at[l.s2], s=l.s1)
-    down_a.step(1)
-    down_b.step(0)
-    down_a.step(2)
-    mid_near.wait_recv()
-    mid_more.wait_recv()
-    for piece in gate_up:
-        piece.finish()
-    units_up(r, l.s3)
-    units_up(r, l.s2)
     down_b.step(1)
-    units_up(r, l.s1)
-    units_up(r, l.s)
-    down_b.step(2)
     cot_near.wait_recv()
     cot_more.wait_recv()
     for t in range(SEQ):
@@ -1005,8 +1028,6 @@
         grad = dot(r.flipped[rows, :], cot).astype(BF)
         r.down_part[pl.ds(2 * k, 2)] = grad.reshape(2, FF_SHARD, WIDTH)
 
-    down_a.finish()
-    l.drain()
     down_a_sum = Scatter(
         l, lambda b: r.down_part.at[b, pl.ds(0, SUM_A)], lambda k: r.down_a_slots.at[k], lambda k: r.down_a_slots.at[4 + k]
     )
@@ -1019,14 +1040,17 @@
     )
     d_mid = RowSum(l, r.slots_a)
     home = []
+    down_a.step(2)
     down_a_sum.start()
     down_b_sum.start()
     down_b_sum.step(0)
+    down_a.finish()
+    down_b.step(2)
+    l.drain()
     r.parts[0] = units_down(r, l.s3).astype(BF).reshape(8, 32, WIDTH)
     d_mid.hand_over(r.parts.at[0])
     r.parts[1] = units_down(r, l.s2).astype(BF).reshape(8, 32, WIDTH)
     d_mid.cross(r.parts.at[1])
-    down_b_sum.step(1)
     r.parts[2] = units_down(r, l.s1).astype(BF).reshape(8, 32, WIDTH)
     d_mid.near(r.parts.at[2])
     r.input_grad[...] = units_down(r, l.s)
@@ -1071,34 +1095,33 @@
         r.att_own[part] = dot_nt(d_branch, rows).astype(BF)
     d_att = [l.push(r.att_own.at[o], r.d_att_rows.at[l.s], s=o) for o in l.others]
     r.d_att_rows[l.s] = r.att_own[l.s]
-    gu_sums[2].start()
+    down_b_sum.step(1)
     down_a_sum.join()
     down_a_sum.step(0)
-    own_gu_sum.step(1)
-    for copy in d_att:
-        copy.wait_recv()
-    l.settle((d_mid.first, d_mid.second, d_mid.third))
-    attention_block_back(r, 0, 3)
     for part in range(SEQ):
         grad = dot_tn(r.att_local[part], d_branch).astype(BF)
         r.out_all[2 * part : 2 * part + 2] = grad.reshape(2, 4, 32, WIDTH)
     out_row = RowSum(l, r.slots_b)
     out_row.hand_over(r.out_all.at[:, l.s3])
+    gu_sums[1].join()
+    gu_sums[1].step(0)
+    gu_sums[2].start()
     out_row.cross(r.out_all.at[:, l.s2])
     out_row.near(r.out_all.at[:, l.s1])
-    gu_sums[0].start()
-    own_gu_sum.step(2)
+    for copy in d_att:
+        copy.wait_recv()
+    l.settle((d_mid.first, d_mid.second, d_mid.third))
+    attention_block_back(r, 0, 3)
     attention_block_back(r, 1, 3)
     attention_block_back(r, 0, 2)
     attention_block_back(r, 1, 2)
+    down_b_sum.step(2)
     attention_block_back(r, 0, 1)
+    own_gu_sum.step(1)
     attention_block_back(r, 1, 1)
     attention_block_back(r, 0, 0)
     attention_block_back(r, 1, 0)
-    gu_sums[1].join()
-    gu_sums[1].step(0)
-    down_b_sum.step(2)
-    down_a_sum.step(1)
+    gu_sums[0].start()
     head_backward(r)
     out_total = out_row.total(r.out_all[:, l.s].astype(F32))
     r.out_all[:, l.s] = out_total.astype(BF)
@@ -1118,25 +1141,20 @@
     r.parts[2] = d_u_part(l.s1).astype(BF).reshape(8, 32, WIDTH)
     d_u.near(r.parts.at[2])
     own = d_u_part(l.s)
-    down_b_sum.cross()
-    gu_sums[1].step(1)
-    down_a_sum.step(2)
+    gu_sums[2].join()
+    gu_sums[2].step(0)
+    down_a_sum.step(1)
     for t in range(SEQ):
         r.flipped[:WIDTH, t * TOK : (t + 1) * TOK] = r.u_rows[t].T
     grad = dot(r.flipped[:WIDTH, :], r.d_qkv[...]).astype(BF)
     r.qkv_all[...] = grad.reshape(8, 4, 32, QKV)
     qkv_sum = Scatter(l, lambda b: r.qkv_all.at[b], lambda k: r.qkv_slots.at[k], lambda k: r.qkv_slots.at[4 + k])
-    gu_sums[2].join()
-    gu_sums[2].step(0)
+    down_a_sum.step(2)
     qkv_sum.start()
-    out_sum.start()
+    gu_sums[1].step(1)
+    own_gu_sum.step(2)
     gu_sums[1].step(2)
-    gu_sums[0].join()
-    gu_sums[0].step(0)
-    r.gu_all[l.dp, l.s2] = gu_sums[1].total().astype(BF)
-    home.append(l.push(r.gu_all.at[l.dp, l.s2], r.gu_grad.at[l.s], s=l.s2))
     gu_sums[2].step(1)
-    own_gu_sum.cross()
     x = r.inputs[...].astype(F32)
     d_values, attn_gain_part = norm_back_unit(d_u.total(own), x)
     r.input_grad[...] += d_values
@@ -1147,14 +1165,15 @@
     r.gains[0, 3:8, :] = jnp.zeros((5, WIDTH), F32)
     gains = [l.push(r.gains.at[0], r.gain_slots.at[k], s=o) for k, o in enumerate(l.others)]
     l.settle((d_u.first, d_u.second, d_u.third))
+    gu_sums[0].join()
+    gu_sums[0].step(0)
+    out_sum.start()
     down_all = r.down_all[...].reshape(FF_OWN, WIDTH)
     last = RowSum(l, r.slots_b)
     r.parts[0] = dot(r.active[l.s3], down_all).astype(BF).reshape(8, 32, WIDTH)
     last.hand_over(r.parts.at[0])
     r.parts[1] = dot(r.active[l.s2], down_all).astype(BF).reshape(8, 32, WIDTH)
     last.cross(r.parts.at[1])
-    gu_sums[2].step(2)
-    gu_sums[0].step(1)
     r.parts[2] = dot(r.active[l.s1], down_all).astype(BF).reshape(8, 32, WIDTH)
     last.near(r.parts.at[2])
     own = r.middle[...] + dot(r.active[l.s], down_all)
@@ -1162,25 +1181,31 @@
         copy.wait_recv()
     r.gains[1] = r.gains[0] + r.gain_slots[0] + r.gain_slots[1] + r.gain_slots[2]
     gains_y = l.push(r.gains.at[1], r.gain_slots.at[3], dp=l.y_peer)
-    gu_sums[0].step(2)
+    gu_sums[2].step(2)
+    gu_sums[0].step(1)
+    down_b_sum.cross()
+    r.down_grad[0:SUM_A] = down_a_sum.total()
     qkv_sum.join()
     qkv_sum.step(0)
+    own_gu_sum.cross()
+    out_sum.join()
+    out_sum.step(0)
+    gu_sums[0].step(2)
     r.gu_all[l.dp, l.s3] = gu_sums[2].total().astype(BF)
     home.append(l.push(r.gu_all.at[l.dp, l.s3], r.gu_grad.at[l.s], s=l.s3))
+    r.gu_all[l.dp, l.s2] = gu_sums[1].total().astype(BF)
+    home.append(l.push(r.gu_all.at[l.dp, l.s2], r.gu_grad.at[l.s], s=l.s2))
+    qkv_sum.step(1)
     r.down_grad[SUM_A:] = down_b_sum.total()
-    qkv_sum.step(1)
     r.gu_all[l.dp, l.s1] = gu_sums[0].total().astype(BF)
     home.append(l.push(r.gu_all.at[l.dp, l.s1], r.gu_grad.at[l.s], s=l.s1))
-    out_sum.join()
-    out_sum.step(0)
     qkv_sum.step(2)
-    r.down_grad[0:SUM_A] = down_a_sum.total()
     r.output[...] = last.total(own).astype(BF)
     gains_y.wait_recv()
     r.gains[2] = r.gains[1] + r.gain_slots[3]
     gains_z = [l.push(r.gains.at[2], r.gain_slots.at[4 + k], dp=p) for k, p in enumerate(l.z_peers)]
+    r.gu_grad[l.s] = own_gu_sum.total().astype(BF)
     out_sum.step(1)
-    r.gu_grad[l.s] = own_gu_sum.total().astype(BF)
     r.qkv_all[l.dp] = qkv_sum.total().astype(BF)
     home += [l.push(r.qkv_all.at[l.dp, o], r.qkv_grad.at[l.s], s=o) for o in l.others]
     r.qkv_grad[l.s] = r.qkv_all[l.dp, l.s]
@@ -1190,6 +1215,7 @@
         copy.wait_recv()
     r.gain_grads[...] = r.gains[2] + r.gain_slots[4] + r.gain_slots[5] + r.gain_slots[6]
     l.drain()
+    l.drain_late()
 
 
 def own_lanes(row, size):
@@ -1197,25 +1223,17 @@
     return pltpu.roll(row, lax.rem(WIDTH - place, WIDTH), 1)[:, :size]
 
 
-def column(row):
-    n = row.shape[1]
-    same = lax.broadcasted_iota(jnp.int32, (n, n), 0) == lax.broadcasted_iota(jnp.int32, (n, n), 1)
-    return jnp.sum(jnp.where(same, row, 0.0), axis=1, keepdims=True)
-
-
 def lay_out(
     output, input_grad, down_grad, out_grad, gu_grad, qkv_grad, gains, attn_gain, ffn_gain,
-    output_o, input_o, attn_o, query_o, key_o, value_o, q_gain_o, k_gain_o, out_o, ffn_o, gate_o, up_o, down_o, sems,
+    output_o, input_o, attn_o, query_o, key_o, value_o, q_gain_o, k_gain_o, out_o, ffn_o, gate_o, up_o, down_o,
 ):
-    pairs = ((output, output_o), (input_grad, input_o), (down_grad, down_o), (out_grad, out_o))
-    copies = [pltpu.make_async_copy(src, dst, sems.at[n]) for n, (src, dst) in enumerate(pairs)]
-    for copy in copies:
-        copy.start()
-    scale = attn_gain[...]
+    for src, dst in ((output, output_o), (input_grad, input_o), (down_grad, down_o), (out_grad, out_o)):
+        dst[...] = src[...]
+    attn_scale = scale = column(as_row(attn_gain))
     for o in range(SEQ):
         for ref, first, size in ((query_o, 0, OWN_Q), (key_o, OWN_Q, OWN_K), (value_o, OWN_Q + OWN_K, OWN_K)):
             ref[:, o * size : (o + 1) * size] = qkv_grad[o, :, first : first + size].astype(F32) * scale
-    scale = ffn_gain[...]
+    scale = column(as_row(ffn_gain))
     for ref, first in ((gate_o, 0), (up_o, FF_OWN)):
         parts = []
         for j in range(8):
@@ -1224,12 +1242,10 @@
                 parts.append(part.astype(F32) * scale)
         ref[...] = jnp.concatenate(parts, axis=1)
     size = attn_o.shape[0]
-    attn_o[...] = (column(own_lanes(gains[0:1, :], size)) / attn_gain[...]).reshape(size)
-    ffn_o[...] = (column(own_lanes(gains[1:2, :], size)) / ffn_gain[...]).reshape(size)
+    attn_o[...] = (column(own_lanes(gains[0:1, :], size)) / attn_scale).reshape(size)
+    ffn_o[...] = (column(own_lanes(gains[1:2, :], size)) / scale).reshape(size)
     q_gain_o[...] = (gains[2:3, 0:64] + gains[2:3, 64:128]).reshape(HEAD_SIZE)
     k_gain_o[...] = (gains[2:3, 128:192] + gains[2:3, 192:256]).reshape(HEAD_SIZE)
-    for copy in copies:
-        copy.wait()
 
 
 class Names:
@@ -1264,10 +1280,10 @@
     given = dict(
         inputs=inputs,
         cotangent=cotangent,
-        attn_gain=attn_gain.astype(F32)[:, None],
-        ffn_gain=ffn_gain.astype(F32)[:, None],
-        q_gain=jnp.tile(q_gain.astype(F32), 2)[None],
-        k_gain=jnp.tile(k_gain.astype(F32), 2)[None],
+        attn_gain=attn_gain,
+        ffn_gain=ffn_gain,
+        q_gain=q_gain,
+        k_gain=k_gain,
         w_query=w_query,
         w_key=key_projection_weight,
         w_value=value_projection_weight,
@@ -1373,12 +1389,9 @@
         pl.pallas_call(
             lay_out,
             out_shape=[jax.ShapeDtypeStruct(*shape) for shape in shapes],
-            in_specs=[pl.BlockSpec(memory_space=pl.ANY)] * 4 + [pl.BlockSpec(memory_space=pltpu.VMEM)] * 5,
-            out_specs=[
-                pl.BlockSpec(memory_space=pl.ANY if n in (0, 1, 8, 12) else pltpu.VMEM) for n in range(13)
-            ],
-            scratch_shapes=[pltpu.SemaphoreType.DMA((4,))],
-            compiler_params=pltpu.CompilerParams(vmem_limit_bytes=24 * 2**20),
+            in_specs=[pl.BlockSpec(memory_space=pltpu.VMEM)] * 9,
+            out_specs=[pl.BlockSpec(memory_space=pltpu.VMEM)] * 13,
+            compiler_params=pltpu.CompilerParams(vmem_limit_bytes=VMEM_BYTES),
             cost_estimate=pl.CostEstimate(flops=1_000_000, bytes_accessed=10_000_000, transcendentals=0),
         )(*done, given["attn_gain"], given["ffn_gain"])
     )

time: 231 us -> 206 us (0.89)
  Pallas kernels: 215 us -> 202 us
  local copies, waits for them, and re-layouts: 10.2 us -> 0 us
    pallas_call x1, Pallas kernels: 212 us -> 197 us  [on_device_in_kernels(): pl.pallas_call(body, out_shape=[jax.ShapeDtypeStruct(*result) for result...]
    unnamed x24 -> x0, local copies, waits for them, and re-layouts: 7.68 us -> none
where the time goes in v3:
time: 206 us; the launch traced here: 203 us
  Pallas kernels  202 us (98%)
    pallas_call x1, Pallas kernels, on_device_in_kernels(): pl.pallas_call(body, out_shape=[jax.ShapeDtypeStruct(*result) for result...  197 us
    pallas_call x1, Pallas kernels, on_device_in_kernels(): pl.pallas_call(lay_out, out_shape=[jax.ShapeDtypeStruct(*shape) for shape...  4.33 us

profile of v3, /device:TPU:0, one launch (start us, length us, event | category | flops | bytes accessed | tf_op | source)
XLA Modules:
  0.0 202.8 jit_solution(9870040114665419202)
XLA Ops:
  0.6 197.4 %shard_map.246 = (bf16[256,1024]{1,0:T(8,128)(2,1)}, f32[256,1024]{1,0:T(8,128)}, f32[144,1024]{1,0:T(8,128)}, f32[32,1024]{1,0:T(8,128)}, bf16[4,32,2304]{2,1,0...) custom-call(bf16[256,1024]{1,0:T(8,128)(2,1)} %refs_0_.1, bf16[256,1024]{1,0:T(8,128)(2,1)} %refs_1_.1, ...), custom_call_target="tpu_custom_call" | custom-call | flops 30000001024 | bytes 10000000 | tf_op jit(solution)/shard_map/pallas_call | solution.py:1354
  198.0 4.3 %shard_map.247 = (bf16[256,1024]{1,0:T(8,128)(2,1)}, f32[256,1024]{1,0:T(8,128)}, f32[32]{0:T(128)}, f32[32,1024]{1,0:T(8,128)}, f32[32,512]{1,0:T(8,128)}, /*in...) custom-call(bf16[256,1024]{1,0:T(8,128)(2,1)} %get-tuple-element.20., ...), custom_call_target="tpu_custom_call" | custom-call | flops 1000000 | bytes 10000000 | tf_op jit(solution)/shard_map/pallas_call | solution.py:1389

commit v4 on v3

--- a/solution.py
+++ b/solution.py
@@ -401,9 +401,11 @@
 
 
 class Links:
-    def __init__(self, send_sems, recv_sems):
-        self.send_sems, self.recv_sems = send_sems, recv_sems
-        self.used = 0
+    def __init__(self, send_sems, recv_sems, local_sems):
+        self.send_sems, self.recv_sems, self.local_sems = send_sems, recv_sems, local_sems
+        self.column_copies = 0
+        self.row_copies = COLUMN_COPIES
+        self.local_copies = []
         self.open = []
         self.late = []
         self.dp = lax.axis_index("dp")
@@ -430,8 +432,12 @@
         return [(self.dp, s) for s in self.others] + self.column()
 
     def plan(self, src, dst, dp=None, s=None):
-        n = self.used
-        self.used += 1
+        if dp is None:
+            n = self.row_copies
+            self.row_copies += 1
+        else:
+            n = self.column_copies
+            self.column_copies += 1
         copy = pltpu.make_async_remote_copy(
             src_ref=src,
             dst_ref=dst,
@@ -449,6 +455,15 @@
         else:
             pl.when(when)(copy.start)
         (self.late if late else self.open).append((copy, when))
+        return copy
+
+    def start_over(self):
+        self.column_copies = 0
+
+    def keep(self, src, dst):
+        copy = pltpu.make_async_copy(src, dst, self.local_sems.at[len(self.local_copies)])
+        copy.start()
+        self.local_copies.append(copy)
         return copy
 
     def settle(self, copies):
@@ -804,14 +819,14 @@
 def own_parts(r):
     scale = column(as_row(r.attn_gain))
     for o in range(SEQ):
-        for ref, first, size in ((r.w_query, 0, OWN_Q), (r.w_key, OWN_Q, OWN_K), (r.w_value, OWN_Q + OWN_K, OWN_K)):
+        for ref, first, size in ((r.wq, 0, OWN_Q), (r.wk, OWN_Q, OWN_K), (r.wv, OWN_Q + OWN_K, OWN_K)):
             part = ref[:, o * size : (o + 1) * size].astype(F32) * scale
             r.w_qkv[o, :, first : first + size] = part.astype(BF)
 
 
 def own_units(r):
     scale = column(as_row(r.ffn_gain))
-    for ref, first in ((r.w_gate, 0), (r.w_up, FF_OWN)):
+    for ref, first in ((r.wg, 0), (r.wu, FF_OWN)):
         scaled = ref[...].astype(F32) * scale
         for o in range(SEQ):
             parts = [scaled[:, (4 * j + o) * FF_SHARD : (4 * j + o + 1) * FF_SHARD] for j in range(8)]
@@ -900,17 +915,27 @@
 
 
 def whole_block(r):
-    l = r.links = Links(r.send_sems, r.recv_sems)
+    l = r.links = Links(r.send_sems, r.recv_sems, r.local_sems)
     l.greet(pltpu.get_barrier_semaphore(), l.everyone())
-    x = r.inputs[...].astype(F32)
+    read = [l.keep(src, dst) for src, dst in ((r.inputs, r.x_own), (r.w_query, r.wq), (r.w_key, r.wk), (r.w_value, r.wv))]
+    read_units = [l.keep(r.w_gate, r.wg), l.keep(r.w_up, r.wu)]
+    read_own = [
+        l.keep(r.w_out, r.out_all.at[l.dp, l.s]),
+        l.keep(r.w_down, r.down_all.at[l.dp]),
+        l.keep(r.cotangent, r.cot_rows.at[l.s]),
+    ]
+    for copy in read:
+        copy.wait()
+    own_parts(r)
+    r.qkv_all[l.dp, l.s] = r.w_qkv[l.s]
+    x = r.x_own[...].astype(F32)
     r.u_rows[l.s] = unit_norm(x).astype(BF)
-    own_parts(r)
+    for copy in read_units:
+        copy.wait()
     own_units(r)
-    r.out_all[l.dp, l.s] = r.w_out[...]
-    r.qkv_all[l.dp, l.s] = r.w_qkv[l.s]
     r.gu_all[l.dp, l.s] = r.d_gu[32 + l.s]
-    r.down_all[l.dp] = r.w_down[...]
-    r.cot_rows[l.s] = r.cotangent[...]
+    for copy in read_own:
+        copy.wait()
     pl.semaphore_wait(pltpu.get_barrier_semaphore(), len(l.everyone()))
     out = PairGather(l, lambda b: r.out_all.at[b, l.s])
     qkv = Gather(l, lambda b: r.qkv_all.at[b])
@@ -918,65 +943,68 @@
     down_a = Gather(l, lambda b: r.down_all.at[b, pl.ds(0, DOWN_A)])
     down_b = PairGather(l, lambda b: r.down_all.at[b, pl.ds(DOWN_A, DOWN_B)])
     qkv_cols = [l.push(r.w_qkv.at[o], r.qkv_all.at[l.dp, l.s], s=o) for o in l.others]
+    out.start_y()
+    u_far = l.push(r.u_rows.at[l.s], r.u_rows.at[l.s], s=l.s2)
+    u_near = l.push(r.u_rows.at[l.s], r.u_rows.at[l.s], s=l.s1)
+    gate_up[0].start_y()
     gate_up[0].start_z()
-    gate_up[0].start_y()
+    down_b.start_y()
     for copy in qkv_cols:
         copy.wait_recv()
     qkv.start_z()
-    out.start_y()
-    gu_cols = [l.push(r.d_gu.at[32 + o], r.gu_all.at[l.dp, l.s], s=o) for o in l.others]
     out.start_z()
     rotation_tables(r, 0)
-    down_b.start_y()
+    out.join()
+    qkv.step(0)
     qkv.start_y()
-    out.join()
-    u_far = l.push(r.u_rows.at[l.s], r.u_rows.at[l.s], s=l.s2)
-    u_near = l.push(r.u_rows.at[l.s], r.u_rows.at[l.s], s=l.s1)
-    qkv.step(0)
+    gu_cols = [l.push(r.d_gu.at[32 + o], r.gu_all.at[l.dp, l.s], s=o) for o in l.others]
+    down_b.start_z()
+    qkv.step(1)
+    gate_up[0].step(0)
+    out.step(0)
+    u_far.wait_recv()
+    u_more = l.push(r.u_rows.at[l.s2], r.u_rows.at[l.s2], s=l.s1)
+    qkv.step(2)
     gu_cols[1].wait_recv()
     gu_cols[2].wait_recv()
+    u_near.wait_recv()
+    u_more.wait_recv()
     gu_cols[0].wait_recv()
-    out.step(0)
+    gate_up[1].start_y()
+    out.step(1)
+    gate_up[1].start_z()
+    gate_up[0].step(1)
+    rotation_tables(r, 1)
     gate_up[2].start_y()
-    rotation_tables(r, 1)
-    out.step(1)
-    gate_up[1].start_y()
-    qkv.step(1)
-    gate_up[1].start_z()
-    u_far.wait_recv()
-    u_more = l.push(r.u_rows.at[l.s2], r.u_rows.at[l.s2], s=l.s1)
+    qkv.finish()
+    head_forward(r)
+    gate_up[3].start_y()
+    gate_up[1].step(0)
     out.step(2)
-    gate_up[3].start_z()
-    qkv.step(2)
-    gate_up[0].step(0)
-    gate_up[3].step(0)
-    gate_up[3].start_y()
-    qkv.finish()
-    gate_up[1].step(0)
+    attention_block(r, 0, 3)
     out_far = l.push(r.out_all.at[:, l.s], r.out_all.at[:, l.s], s=l.s2)
     out_near = l.push(r.out_all.at[:, l.s], r.out_all.at[:, l.s], s=l.s1)
-    u_near.wait_recv()
-    u_more.wait_recv()
-    gate_up[0].step(1)
-    head_forward(r)
-    down_a.start_z()
-    attention_block(r, 0, 3)
+    gate_up[3].start_z()
+    gate_up[2].start_z()
     attention_block(r, 1, 3)
+    gate_up[0].step(2)
     attention_block(r, 0, 2)
     attention_block(r, 1, 2)
+    gate_up[3].step(0)
     attention_block(r, 0, 1)
-    gate_up[0].step(2)
-    gate_up[3].step(1)
+    gate_up[1].step(1)
     attention_block(r, 1, 1)
-    gate_up[2].start_z()
     attention_block(r, 0, 0)
     attention_block(r, 1, 0)
     att = [l.push(r.att_own.at[o], r.att_local.at[l.s], s=o) for o in l.others]
     r.att_local[l.s] = r.att_own[l.s]
-    gate_up[3].step(2)
-    gate_up[1].step(1)
+    gate_up[0].finish()
     out_far.wait_recv()
     out_more = l.push(r.out_all.at[:, l.s2], r.out_all.at[:, l.s2], s=l.s1)
+    gate_up[3].step(1)
+    gate_up[2].step(0)
+    down_a.start_z()
+    gate_up[1].step(2)
     out_near.wait_recv()
     out_more.wait_recv()
     for copy in att:
@@ -989,33 +1017,31 @@
     r.mid_rows[l.s] = unit_norm(middle).astype(BF)
     mid_far = l.push(r.mid_rows.at[l.s], r.mid_rows.at[l.s], s=l.s2)
     mid_near = l.push(r.mid_rows.at[l.s], r.mid_rows.at[l.s], s=l.s1)
-    down_b.start_z()
-    gate_up[1].step(2)
+    gate_up[2].step(1)
+    down_b.join()
+    gate_up[3].step(2)
+    gate_up[2].step(2)
+    down_a.start_y()
+    down_a.step(0)
     cot_far = l.push(r.cot_rows.at[l.s], r.cot_rows.at[l.s], s=l.s2)
     cot_near = l.push(r.cot_rows.at[l.s], r.cot_rows.at[l.s], s=l.s1)
-    gate_up[2].step(0)
-    gate_up[2].step(1)
-    gate_up[2].step(2)
-    down_b.join()
-    down_a.start_y()
-    gate_up[1].finish()
-    gate_up[3].finish()
+    down_a.step(1)
     mid_far.wait_recv()
     mid_more = l.push(r.mid_rows.at[l.s2], r.mid_rows.at[l.s2], s=l.s1)
     mid_near.wait_recv()
     mid_more.wait_recv()
-    down_a.step(0)
+    gate_up[2].finish()
+    gate_up[3].finish()
+    gate_up[1].finish()
+    units_up(r, l.s3)
     down_b.step(0)
-    gate_up[0].finish()
-    gate_up[2].finish()
-    units_up(r, l.s3)
-    down_a.step(1)
     units_up(r, l.s2)
     units_up(r, l.s1)
+    down_a.step(2)
     units_up(r, l.s)
+    down_b.step(1)
     cot_far.wait_recv()
     cot_more = l.push(r.cot_rows.at[l.s2], r.cot_rows.at[l.s2], s=l.s1)
-    down_b.step(1)
     cot_near.wait_recv()
     cot_more.wait_recv()
     for t in range(SEQ):
@@ -1040,7 +1066,7 @@
     )
     d_mid = RowSum(l, r.slots_a)
     home = []
-    down_a.step(2)
+    kept = []
     down_a_sum.start()
     down_b_sum.start()
     down_b_sum.step(0)
@@ -1053,7 +1079,7 @@
     d_mid.cross(r.parts.at[1])
     r.parts[2] = units_down(r, l.s1).astype(BF).reshape(8, 32, WIDTH)
     d_mid.near(r.parts.at[2])
-    r.input_grad[...] = units_down(r, l.s)
+    r.d_input[...] = units_down(r, l.s)
     for t in range(SEQ):
         r.flipped[:WIDTH, t * TOK : (t + 1) * TOK] = r.mid_rows[t].T
     d_gu = r.d_gu[0:32].reshape(ROW, HIDDEN_TWO)
@@ -1066,6 +1092,7 @@
 
     l.greet(r.free, l.column())
     pl.semaphore_wait(r.free, len(l.column()))
+    l.start_over()
     gu_sums = [
         Scatter(
             l,
@@ -1082,12 +1109,13 @@
         lambda k: r.d_gu.at[27 + k],
         lambda k: r.d_gu.at[32 + k],
     )
-    own_gu_sum.start()
-    own_gu_sum.step(0)
-    gu_sums[1].start()
-    d_values, ffn_gain_part = norm_back_unit(d_mid.total(r.input_grad[...]), r.middle[...])
-    d_middle = r.cotangent[...].astype(F32) + d_values
-    r.input_grad[...] = d_middle
+    down_a_sum.join()
+    down_a_sum.step(0)
+    down_b_sum.step(1)
+    gu_sums[2].start()
+    d_values, ffn_gain_part = norm_back_unit(d_mid.total(r.d_input[...]), r.middle[...])
+    d_middle = r.cot_rows[l.s].astype(F32) + d_values
+    r.d_input[...] = d_middle
     d_branch = d_middle.astype(BF)
     r.gains[0, 1:2, :] = ffn_gain_part
     for part in range(SEQ):
@@ -1095,39 +1123,41 @@
         r.att_own[part] = dot_nt(d_branch, rows).astype(BF)
     d_att = [l.push(r.att_own.at[o], r.d_att_rows.at[l.s], s=o) for o in l.others]
     r.d_att_rows[l.s] = r.att_own[l.s]
-    down_b_sum.step(1)
-    down_a_sum.join()
-    down_a_sum.step(0)
+    own_gu_sum.start()
+    own_gu_sum.step(0)
     for part in range(SEQ):
         grad = dot_tn(r.att_local[part], d_branch).astype(BF)
         r.out_all[2 * part : 2 * part + 2] = grad.reshape(2, 4, 32, WIDTH)
     out_row = RowSum(l, r.slots_b)
     out_row.hand_over(r.out_all.at[:, l.s3])
-    gu_sums[1].join()
-    gu_sums[1].step(0)
-    gu_sums[2].start()
     out_row.cross(r.out_all.at[:, l.s2])
     out_row.near(r.out_all.at[:, l.s1])
     for copy in d_att:
         copy.wait_recv()
     l.settle((d_mid.first, d_mid.second, d_mid.third))
+    gu_sums[1].start()
+    gu_sums[0].start()
+    down_b_sum.step(2)
     attention_block_back(r, 0, 3)
     attention_block_back(r, 1, 3)
     attention_block_back(r, 0, 2)
     attention_block_back(r, 1, 2)
-    down_b_sum.step(2)
+    down_a_sum.step(1)
     attention_block_back(r, 0, 1)
-    own_gu_sum.step(1)
+    gu_sums[2].join()
+    gu_sums[2].step(0)
     attention_block_back(r, 1, 1)
+    down_b_sum.cross()
     attention_block_back(r, 0, 0)
-    attention_block_back(r, 1, 0)
-    gu_sums[0].start()
-    head_backward(r)
     out_total = out_row.total(r.out_all[:, l.s].astype(F32))
     r.out_all[:, l.s] = out_total.astype(BF)
     out_sum = Scatter(
         l, lambda b: r.out_all.at[b, l.s], lambda k: r.out_slots.at[k], lambda k: r.out_slots.at[4 + k]
     )
+    attention_block_back(r, 1, 0)
+    own_gu_sum.step(1)
+    head_backward(r)
+    down_a_sum.step(2)
     d_u = RowSum(l, r.slots_a)
     weights = r.qkv_all[...].reshape(WIDTH, QKV)
 
@@ -1141,23 +1171,23 @@
     r.parts[2] = d_u_part(l.s1).astype(BF).reshape(8, 32, WIDTH)
     d_u.near(r.parts.at[2])
     own = d_u_part(l.s)
-    gu_sums[2].join()
-    gu_sums[2].step(0)
-    down_a_sum.step(1)
     for t in range(SEQ):
         r.flipped[:WIDTH, t * TOK : (t + 1) * TOK] = r.u_rows[t].T
     grad = dot(r.flipped[:WIDTH, :], r.d_qkv[...]).astype(BF)
     r.qkv_all[...] = grad.reshape(8, 4, 32, QKV)
     qkv_sum = Scatter(l, lambda b: r.qkv_all.at[b], lambda k: r.qkv_slots.at[k], lambda k: r.qkv_slots.at[4 + k])
-    down_a_sum.step(2)
+    own_gu_sum.step(2)
+    gu_sums[1].join()
+    gu_sums[1].step(0)
     qkv_sum.start()
+    gu_sums[2].step(1)
     gu_sums[1].step(1)
-    own_gu_sum.step(2)
-    gu_sums[1].step(2)
-    gu_sums[2].step(1)
-    x = r.inputs[...].astype(F32)
+    gu_sums[0].join()
+    gu_sums[0].step(0)
+    x = r.x_own[...].astype(F32)
     d_values, attn_gain_part = norm_back_unit(d_u.total(own), x)
-    r.input_grad[...] += d_values
+    r.d_input[...] += d_values
+    kept.append(l.keep(r.d_input, r.input_grad))
     r.gains[0, 0:1, :] = attn_gain_part
     r.gains[0, 2:3, 0:128] = r.head_gain_part[0:1]
     r.gains[0, 2:3, 128:256] = r.head_gain_part[1:2]
@@ -1165,15 +1195,19 @@
     r.gains[0, 3:8, :] = jnp.zeros((5, WIDTH), F32)
     gains = [l.push(r.gains.at[0], r.gain_slots.at[k], s=o) for k, o in enumerate(l.others)]
     l.settle((d_u.first, d_u.second, d_u.third))
-    gu_sums[0].join()
-    gu_sums[0].step(0)
-    out_sum.start()
     down_all = r.down_all[...].reshape(FF_OWN, WIDTH)
     last = RowSum(l, r.slots_b)
     r.parts[0] = dot(r.active[l.s3], down_all).astype(BF).reshape(8, 32, WIDTH)
     last.hand_over(r.parts.at[0])
     r.parts[1] = dot(r.active[l.s2], down_all).astype(BF).reshape(8, 32, WIDTH)
     last.cross(r.parts.at[1])
+    own_gu_sum.cross()
+    gu_sums[1].step(2)
+    qkv_sum.join()
+    qkv_sum.step(0)
+    gu_sums[0].step(1)
+    out_sum.start()
+    gu_sums[2].step(2)
     r.parts[2] = dot(r.active[l.s1], down_all).astype(BF).reshape(8, 32, WIDTH)
     last.near(r.parts.at[2])
     own = r.middle[...] + dot(r.active[l.s], down_all)
@@ -1181,38 +1215,39 @@
         copy.wait_recv()
     r.gains[1] = r.gains[0] + r.gain_slots[0] + r.gain_slots[1] + r.gain_slots[2]
     gains_y = l.push(r.gains.at[1], r.gain_slots.at[3], dp=l.y_peer)
-    gu_sums[2].step(2)
-    gu_sums[0].step(1)
-    down_b_sum.cross()
-    r.down_grad[0:SUM_A] = down_a_sum.total()
-    qkv_sum.join()
-    qkv_sum.step(0)
-    own_gu_sum.cross()
-    out_sum.join()
-    out_sum.step(0)
     gu_sums[0].step(2)
-    r.gu_all[l.dp, l.s3] = gu_sums[2].total().astype(BF)
-    home.append(l.push(r.gu_all.at[l.dp, l.s3], r.gu_grad.at[l.s], s=l.s3))
     r.gu_all[l.dp, l.s2] = gu_sums[1].total().astype(BF)
     home.append(l.push(r.gu_all.at[l.dp, l.s2], r.gu_grad.at[l.s], s=l.s2))
     qkv_sum.step(1)
-    r.down_grad[SUM_A:] = down_b_sum.total()
+    out_sum.join()
+    out_sum.step(0)
+    r.gu_all[l.dp, l.s3] = gu_sums[2].total().astype(BF)
+    home.append(l.push(r.gu_all.at[l.dp, l.s3], r.gu_grad.at[l.s], s=l.s3))
+    r.down_own[0:SUM_A] = down_a_sum.total()
+    kept.append(l.keep(r.down_own.at[pl.ds(0, SUM_A)], r.down_grad.at[pl.ds(0, SUM_A)]))
+    qkv_sum.step(2)
+    r.gu_all[l.dp, l.s] = own_gu_sum.total().astype(BF)
+    kept.append(l.keep(r.gu_all.at[l.dp, l.s], r.gu_grad.at[l.s]))
     r.gu_all[l.dp, l.s1] = gu_sums[0].total().astype(BF)
     home.append(l.push(r.gu_all.at[l.dp, l.s1], r.gu_grad.at[l.s], s=l.s1))
-    qkv_sum.step(2)
-    r.output[...] = last.total(own).astype(BF)
+    out_sum.step(1)
+    r.output_own[...] = last.total(own).astype(BF)
+    kept.append(l.keep(r.output_own, r.output))
     gains_y.wait_recv()
     r.gains[2] = r.gains[1] + r.gain_slots[3]
     gains_z = [l.push(r.gains.at[2], r.gain_slots.at[4 + k], dp=p) for k, p in enumerate(l.z_peers)]
-    r.gu_grad[l.s] = own_gu_sum.total().astype(BF)
-    out_sum.step(1)
     r.qkv_all[l.dp] = qkv_sum.total().astype(BF)
     home += [l.push(r.qkv_all.at[l.dp, o], r.qkv_grad.at[l.s], s=o) for o in l.others]
-    r.qkv_grad[l.s] = r.qkv_all[l.dp, l.s]
+    kept.append(l.keep(r.qkv_all.at[l.dp, l.s], r.qkv_grad.at[l.s]))
     out_sum.step(2)
-    r.out_grad[...] = out_sum.total()
+    r.down_own[SUM_A:] = down_b_sum.total()
+    kept.append(l.keep(r.down_own.at[pl.ds(SUM_A, SUM_B)], r.down_grad.at[pl.ds(SUM_A, SUM_B)]))
+    r.out_own[...] = out_sum.total()
+    kept.append(l.keep(r.out_own, r.out_grad))
     for copy in gains_z + home:
         copy.wait_recv()
+    for copy in kept:
+        copy.wait()
     r.gain_grads[...] = r.gains[2] + r.gain_slots[4] + r.gain_slots[5] + r.gain_slots[6]
     l.drain()
     l.drain_late()
@@ -1257,7 +1292,9 @@
     return jnp.asarray(np.tile(THETA ** (-steps), 4)[None], F32)
 
 
-MAX_COPIES = 300
+COLUMN_COPIES = 126
+ROW_COPIES = 45
+LOCAL_COPIES = 16
 VMEM_BYTES = 63 * 2**20
 
 
@@ -1304,6 +1341,16 @@
         gain_grads=((8, WIDTH), F32),
     )
     kept = dict(
+        x_own=((TOK, WIDTH), BF),
+        wq=((32, SEQ * OWN_Q), BF),
+        wk=((32, SEQ * OWN_K), BF),
+        wv=((32, SEQ * OWN_K), BF),
+        wg=((32, FF), BF),
+        wu=((32, FF), BF),
+        output_own=((TOK, WIDTH), BF),
+        d_input=((TOK, WIDTH), F32),
+        down_own=((FF_SHARD, WIDTH), F32),
+        out_own=((32, WIDTH), F32),
         w_qkv=((SEQ, 32, QKV), BF),
         cosine=((ROW, 128), F32),
         sine=((ROW, 128), F32),
@@ -1348,20 +1395,22 @@
         names = [*given, *results, *kept]
         for name, ref in zip(names, refs):
             setattr(r, name, ref)
-        r.send_sems, r.recv_sems, r.free = refs[len(names) :]
+        r.send_sems, r.recv_sems, r.local_sems, r.free = refs[len(names) :]
         whole_block(r)
 
     done = pl.pallas_call(
         body,
         out_shape=[jax.ShapeDtypeStruct(*result) for result in results.values()],
         in_specs=[
-            pl.BlockSpec(memory_space=pltpu.SMEM if a is doc_starts else pltpu.VMEM) for a in given.values()
+            pl.BlockSpec(memory_space=pltpu.SMEM if a is doc_starts else pltpu.VMEM if a.size < 1024 else pl.ANY)
+            for a in given.values()
         ],
-        out_specs=[pl.BlockSpec(memory_space=pltpu.VMEM)] * len(results),
+        out_specs=[pl.BlockSpec(memory_space=pl.ANY)] * (len(results) - 1) + [pl.BlockSpec(memory_space=pltpu.VMEM)],
         scratch_shapes=[pltpu.VMEM(*shape) for shape in kept.values()]
         + [
-            pltpu.SemaphoreType.DMA((MAX_COPIES,)),
-            pltpu.SemaphoreType.DMA((MAX_COPIES,)),
+            pltpu.SemaphoreType.DMA((COLUMN_COPIES + ROW_COPIES,)),
+            pltpu.SemaphoreType.DMA((COLUMN_COPIES + ROW_COPIES,)),
+            pltpu.SemaphoreType.DMA((LOCAL_COPIES,)),
             pltpu.SemaphoreType.REGULAR,
         ],
         compiler_params=pltpu.CompilerParams(

time: 206 us -> 200 us (0.971)
  Pallas kernels: 202 us -> 196 us
    pallas_call x1, Pallas kernels: 197 us -> 191 us  [on_device_in_kernels(): pl.pallas_call(body, out_shape=[jax.ShapeDtypeStruct(*result) for result...]
where the time goes in v4:
time: 200 us; the launch traced here: 197 us
  Pallas kernels  196 us (98%)
    pallas_call x1, Pallas kernels, on_device_in_kernels(): pl.pallas_call(body, out_shape=[jax.ShapeDtypeStruct(*result) for result...  191 us
    pallas_call x1, Pallas kernels, on_device_in_kernels(): pl.pallas_call(lay_out, out_shape=[jax.ShapeDtypeStruct(*shape) for shape...  4.33 us

profile of v4, /device:TPU:0, one launch (start us, length us, event | category | flops | bytes accessed | tf_op | source)
XLA Modules:
  0.0 196.6 jit_solution(2165893396373509801)
XLA Ops:
  0.6 191.5 %shard_map.246 = (bf16[256,1024]{1,0:T(8,128)(2,1)}, f32[256,1024]{1,0:T(8,128)}, f32[144,1024]{1,0:T(8,128)}, f32[32,1024]{1,0:T(8,128)}, bf16[4,32,2304]{2,1,0...) custom-call(bf16[256,1024]{1,0:T(8,128)(2,1)} %refs_0_.1, bf16[256,1024]{1,0:T(8,128)(2,1)} %refs_1_.1, ...), custom_call_target="tpu_custom_call" | custom-call | flops 30000001024 | bytes 10000000 | tf_op jit(solution)/shard_map/pallas_call | solution.py:1401
  192.1 4.3 %shard_map.247 = (bf16[256,1024]{1,0:T(8,128)(2,1)}, f32[256,1024]{1,0:T(8,128)}, f32[32]{0:T(128)}, f32[32,1024]{1,0:T(8,128)}, f32[32,512]{1,0:T(8,128)}, /*in...) custom-call(bf16[256,1024]{1,0:T(8,128)(2,1)} %get-tuple-element.20., ...), custom_call_target="tpu_custom_call" | custom-call | flops 1000000 | bytes 10000000 | tf_op jit(solution)/shard_map/pallas_call | solution.py:1438

commit v5 on v4

--- a/solution.py
+++ b/solution.py
@@ -788,11 +788,12 @@
         r.d_kv[pair, :keys, HEAD_SIZE:] += d_value
 
 
-def norm_back_unit(upstream, values):
+def norm_back_row(upstream, values, gain):
     inverse = lax.rsqrt(jnp.mean(values * values, axis=-1, keepdims=True) + EPS)
     unit = values * inverse
+    scaled = upstream * gain
     d_values = inverse * (
-        upstream - unit * jnp.mean(upstream * unit, axis=-1, keepdims=True)
+        scaled - unit * jnp.mean(scaled * unit, axis=-1, keepdims=True)
     )
     return d_values, jnp.sum(upstream * unit, axis=0, keepdims=True)
 
@@ -810,24 +811,32 @@
     return jnp.concatenate([row, row], axis=1)
 
 
-def column(row):
-    n = row.shape[1]
-    same = lax.broadcasted_iota(jnp.int32, (n, n), 0) == lax.broadcasted_iota(jnp.int32, (n, n), 1)
-    return jnp.sum(jnp.where(same, row, 0.0), axis=1, keepdims=True)
-
-
 def own_parts(r):
-    scale = column(as_row(r.attn_gain))
     for o in range(SEQ):
         for ref, first, size in ((r.wq, 0, OWN_Q), (r.wk, OWN_Q, OWN_K), (r.wv, OWN_Q + OWN_K, OWN_K)):
-            part = ref[:, o * size : (o + 1) * size].astype(F32) * scale
-            r.w_qkv[o, :, first : first + size] = part.astype(BF)
+            r.w_qkv[o, :, first : first + size] = ref[:, o * size : (o + 1) * size]
+
+
+def own_gains(r):
+    size = r.attn_gain.shape[0]
+    rest = jnp.zeros((1, 128 - size), F32)
+    place = r.links.s * size
+    rows = [pltpu.roll(jnp.concatenate([as_row(gain), rest], axis=1), place, 1) for gain in (r.attn_gain, r.ffn_gain)]
+    row = lax.broadcasted_iota(jnp.int32, (16, 128), 0)
+    return jnp.where(row == 0, rows[0], jnp.where(row == 1, rows[1], 0.0)).astype(BF)
+
+
+def all_gains(r):
+    for b in range(2 * PLANES):
+        total = r.gain_all[b, 0].astype(F32)
+        for o in range(1, SEQ):
+            total = total + r.gain_all[b, o].astype(F32)
+        r.gain_rows[:, b * 128 : (b + 1) * 128] = total[0:8]
 
 
 def own_units(r):
-    scale = column(as_row(r.ffn_gain))
     for ref, first in ((r.wg, 0), (r.wu, FF_OWN)):
-        scaled = ref[...].astype(F32) * scale
+        scaled = ref[...].astype(F32)
         for o in range(SEQ):
             parts = [scaled[:, (4 * j + o) * FF_SHARD : (4 * j + o + 1) * FF_SHARD] for j in range(8)]
             r.d_gu[32 + o, :, first : first + FF_OWN] = jnp.concatenate(parts, axis=1).astype(BF)
@@ -928,8 +937,7 @@
         copy.wait()
     own_parts(r)
     r.qkv_all[l.dp, l.s] = r.w_qkv[l.s]
-    x = r.x_own[...].astype(F32)
-    r.u_rows[l.s] = unit_norm(x).astype(BF)
+    r.gain_all[l.dp, l.s] = own_gains(r)
     for copy in read_units:
         copy.wait()
     own_units(r)
@@ -942,69 +950,82 @@
     gate_up = [Gather(l, lambda b, g=g: r.gu_all.at[b, g]) for g in (l.s,) + l.others]
     down_a = Gather(l, lambda b: r.down_all.at[b, pl.ds(0, DOWN_A)])
     down_b = PairGather(l, lambda b: r.down_all.at[b, pl.ds(DOWN_A, DOWN_B)])
+    gain_z = [
+        l.push(r.gain_all.at[l.dp, l.s], r.gain_all.at[l.dp, l.s], dp=p) for p in l.z_peers
+    ]
+    gain_y = [l.push(r.gain_all.at[l.dp, l.s], r.gain_all.at[l.dp, l.s], dp=l.y_peer)]
     qkv_cols = [l.push(r.w_qkv.at[o], r.qkv_all.at[l.dp, l.s], s=o) for o in l.others]
     out.start_y()
-    u_far = l.push(r.u_rows.at[l.s], r.u_rows.at[l.s], s=l.s2)
-    u_near = l.push(r.u_rows.at[l.s], r.u_rows.at[l.s], s=l.s1)
     gate_up[0].start_y()
     gate_up[0].start_z()
-    down_b.start_y()
+    for copy, p in zip(gain_z, l.z_peers):
+        copy.wait_recv()
+        gain_y.append(l.push(r.gain_all.at[p, l.s], r.gain_all.at[p, l.s], dp=l.y_peer))
     for copy in qkv_cols:
         copy.wait_recv()
     qkv.start_z()
     out.start_z()
+    down_a.start_y()
+    gu_cols = [l.push(r.d_gu.at[32 + o], r.gu_all.at[l.dp, l.s], s=o) for o in l.others]
+    qkv.start_y()
+    for copy in gain_y:
+        copy.wait_recv()
+    gain_row = [l.push(r.gain_all.at[:, l.s], r.gain_all.at[:, l.s], s=o) for o in l.others]
+    out.join()
     rotation_tables(r, 0)
-    out.join()
     qkv.step(0)
-    qkv.start_y()
-    gu_cols = [l.push(r.d_gu.at[32 + o], r.gu_all.at[l.dp, l.s], s=o) for o in l.others]
+    for copy in gain_row:
+        copy.wait_recv()
+    all_gains(r)
+    x = r.x_own[...].astype(F32)
+    r.u_rows[l.s] = (unit_norm(x) * r.gain_rows[0:1, :]).astype(BF)
+    u_far = l.push(r.u_rows.at[l.s], r.u_rows.at[l.s], s=l.s2)
+    u_near = l.push(r.u_rows.at[l.s], r.u_rows.at[l.s], s=l.s1)
+    out.step(0)
+    gu_cols[1].wait_recv()
+    gu_cols[2].wait_recv()
+    qkv.step(1)
+    gu_cols[0].wait_recv()
+    out.step(1)
+    gate_up[0].step(0)
+    down_a.start_z()
+    gate_up[1].start_z()
+    rotation_tables(r, 1)
     down_b.start_z()
-    qkv.step(1)
-    gate_up[0].step(0)
-    out.step(0)
+    qkv.step(2)
+    gate_up[3].start_y()
+    gate_up[2].start_y()
     u_far.wait_recv()
     u_more = l.push(r.u_rows.at[l.s2], r.u_rows.at[l.s2], s=l.s1)
-    qkv.step(2)
-    gu_cols[1].wait_recv()
-    gu_cols[2].wait_recv()
+    out.step(2)
+    down_b.start_y()
     u_near.wait_recv()
     u_more.wait_recv()
-    gu_cols[0].wait_recv()
-    gate_up[1].start_y()
-    out.step(1)
-    gate_up[1].start_z()
-    gate_up[0].step(1)
-    rotation_tables(r, 1)
-    gate_up[2].start_y()
     qkv.finish()
     head_forward(r)
-    gate_up[3].start_y()
-    gate_up[1].step(0)
-    out.step(2)
     attention_block(r, 0, 3)
+    gate_up[1].start_y()
+    attention_block(r, 1, 3)
     out_far = l.push(r.out_all.at[:, l.s], r.out_all.at[:, l.s], s=l.s2)
     out_near = l.push(r.out_all.at[:, l.s], r.out_all.at[:, l.s], s=l.s1)
     gate_up[3].start_z()
-    gate_up[2].start_z()
-    attention_block(r, 1, 3)
-    gate_up[0].step(2)
+    gate_up[1].step(0)
     attention_block(r, 0, 2)
     attention_block(r, 1, 2)
+    attention_block(r, 0, 1)
+    gate_up[0].step(1)
     gate_up[3].step(0)
-    attention_block(r, 0, 1)
-    gate_up[1].step(1)
     attention_block(r, 1, 1)
     attention_block(r, 0, 0)
     attention_block(r, 1, 0)
     att = [l.push(r.att_own.at[o], r.att_local.at[l.s], s=o) for o in l.others]
     r.att_local[l.s] = r.att_own[l.s]
-    gate_up[0].finish()
+    gate_up[1].step(1)
     out_far.wait_recv()
     out_more = l.push(r.out_all.at[:, l.s2], r.out_all.at[:, l.s2], s=l.s1)
+    gate_up[0].step(2)
     gate_up[3].step(1)
-    gate_up[2].step(0)
-    down_a.start_z()
-    gate_up[1].step(2)
+    gate_up[2].start_z()
     out_near.wait_recv()
     out_more.wait_recv()
     for copy in att:
@@ -1014,34 +1035,36 @@
         rows = r.out_all[part * 2 : (part + 1) * 2].reshape(OWN_Q, WIDTH)
         middle = middle + dot(r.att_local[part], rows)
     r.middle[...] = middle
-    r.mid_rows[l.s] = unit_norm(middle).astype(BF)
+    r.mid_rows[l.s] = (unit_norm(middle) * r.gain_rows[1:2, :]).astype(BF)
     mid_far = l.push(r.mid_rows.at[l.s], r.mid_rows.at[l.s], s=l.s2)
     mid_near = l.push(r.mid_rows.at[l.s], r.mid_rows.at[l.s], s=l.s1)
-    gate_up[2].step(1)
-    down_b.join()
-    gate_up[3].step(2)
-    gate_up[2].step(2)
-    down_a.start_y()
-    down_a.step(0)
     cot_far = l.push(r.cot_rows.at[l.s], r.cot_rows.at[l.s], s=l.s2)
     cot_near = l.push(r.cot_rows.at[l.s], r.cot_rows.at[l.s], s=l.s1)
-    down_a.step(1)
+    gate_up[3].step(2)
+    gate_up[2].step(0)
+    down_b.join()
+    gate_up[2].step(1)
+    gate_up[1].step(2)
+    gate_up[2].step(2)
+    down_a.step(0)
+    down_b.step(0)
     mid_far.wait_recv()
     mid_more = l.push(r.mid_rows.at[l.s2], r.mid_rows.at[l.s2], s=l.s1)
     mid_near.wait_recv()
     mid_more.wait_recv()
-    gate_up[2].finish()
     gate_up[3].finish()
     gate_up[1].finish()
+    down_a.step(1)
+    gate_up[0].finish()
+    gate_up[2].finish()
     units_up(r, l.s3)
-    down_b.step(0)
     units_up(r, l.s2)
+    down_b.step(1)
     units_up(r, l.s1)
-    down_a.step(2)
     units_up(r, l.s)
-    down_b.step(1)
     cot_far.wait_recv()
     cot_more = l.push(r.cot_rows.at[l.s2], r.cot_rows.at[l.s2], s=l.s1)
+    down_a.step(2)
     cot_near.wait_recv()
     cot_more.wait_recv()
     for t in range(SEQ):
@@ -1067,12 +1090,12 @@
     d_mid = RowSum(l, r.slots_a)
     home = []
     kept = []
-    down_a_sum.start()
     down_b_sum.start()
     down_b_sum.step(0)
+    down_b.step(2)
     down_a.finish()
-    down_b.step(2)
     l.drain()
+    down_a_sum.start()
     r.parts[0] = units_down(r, l.s3).astype(BF).reshape(8, 32, WIDTH)
     d_mid.hand_over(r.parts.at[0])
     r.parts[1] = units_down(r, l.s2).astype(BF).reshape(8, 32, WIDTH)
@@ -1109,11 +1132,10 @@
         lambda k: r.d_gu.at[27 + k],
         lambda k: r.d_gu.at[32 + k],
     )
-    down_a_sum.join()
-    down_a_sum.step(0)
-    down_b_sum.step(1)
-    gu_sums[2].start()
-    d_values, ffn_gain_part = norm_back_unit(d_mid.total(r.d_input[...]), r.middle[...])
+    gu_sums[1].start()
+    own_gu_sum.start()
+    own_gu_sum.step(0)
+    d_values, ffn_gain_part = norm_back_row(d_mid.total(r.d_input[...]), r.middle[...], r.gain_rows[1:2, :])
     d_middle = r.cot_rows[l.s].astype(F32) + d_values
     r.d_input[...] = d_middle
     d_branch = d_middle.astype(BF)
@@ -1123,31 +1145,31 @@
         r.att_own[part] = dot_nt(d_branch, rows).astype(BF)
     d_att = [l.push(r.att_own.at[o], r.d_att_rows.at[l.s], s=o) for o in l.others]
     r.d_att_rows[l.s] = r.att_own[l.s]
-    own_gu_sum.start()
-    own_gu_sum.step(0)
     for part in range(SEQ):
         grad = dot_tn(r.att_local[part], d_branch).astype(BF)
         r.out_all[2 * part : 2 * part + 2] = grad.reshape(2, 4, 32, WIDTH)
     out_row = RowSum(l, r.slots_b)
     out_row.hand_over(r.out_all.at[:, l.s3])
+    gu_sums[0].start()
     out_row.cross(r.out_all.at[:, l.s2])
     out_row.near(r.out_all.at[:, l.s1])
+    down_b_sum.step(1)
     for copy in d_att:
         copy.wait_recv()
     l.settle((d_mid.first, d_mid.second, d_mid.third))
-    gu_sums[1].start()
-    gu_sums[0].start()
-    down_b_sum.step(2)
+    gu_sums[2].start()
     attention_block_back(r, 0, 3)
+    gu_sums[1].join()
+    gu_sums[1].step(0)
     attention_block_back(r, 1, 3)
     attention_block_back(r, 0, 2)
+    down_a_sum.join()
+    down_a_sum.step(0)
+    own_gu_sum.step(1)
     attention_block_back(r, 1, 2)
-    down_a_sum.step(1)
+    down_b_sum.step(2)
     attention_block_back(r, 0, 1)
-    gu_sums[2].join()
-    gu_sums[2].step(0)
     attention_block_back(r, 1, 1)
-    down_b_sum.cross()
     attention_block_back(r, 0, 0)
     out_total = out_row.total(r.out_all[:, l.s].astype(F32))
     r.out_all[:, l.s] = out_total.astype(BF)
@@ -1155,9 +1177,8 @@
         l, lambda b: r.out_all.at[b, l.s], lambda k: r.out_slots.at[k], lambda k: r.out_slots.at[4 + k]
     )
     attention_block_back(r, 1, 0)
-    own_gu_sum.step(1)
     head_backward(r)
-    down_a_sum.step(2)
+    gu_sums[1].step(1)
     d_u = RowSum(l, r.slots_a)
     weights = r.qkv_all[...].reshape(WIDTH, QKV)
 
@@ -1171,21 +1192,22 @@
     r.parts[2] = d_u_part(l.s1).astype(BF).reshape(8, 32, WIDTH)
     d_u.near(r.parts.at[2])
     own = d_u_part(l.s)
+    out_sum.start()
+    gu_sums[0].join()
+    gu_sums[0].step(0)
+    gu_sums[2].join()
+    gu_sums[2].step(0)
     for t in range(SEQ):
         r.flipped[:WIDTH, t * TOK : (t + 1) * TOK] = r.u_rows[t].T
     grad = dot(r.flipped[:WIDTH, :], r.d_qkv[...]).astype(BF)
     r.qkv_all[...] = grad.reshape(8, 4, 32, QKV)
     qkv_sum = Scatter(l, lambda b: r.qkv_all.at[b], lambda k: r.qkv_slots.at[k], lambda k: r.qkv_slots.at[4 + k])
+    qkv_sum.start()
+    down_a_sum.step(1)
     own_gu_sum.step(2)
-    gu_sums[1].join()
-    gu_sums[1].step(0)
-    qkv_sum.start()
-    gu_sums[2].step(1)
-    gu_sums[1].step(1)
-    gu_sums[0].join()
-    gu_sums[0].step(0)
+    gu_sums[0].step(1)
     x = r.x_own[...].astype(F32)
-    d_values, attn_gain_part = norm_back_unit(d_u.total(own), x)
+    d_values, attn_gain_part = norm_back_row(d_u.total(own), x, r.gain_rows[0:1, :])
     r.d_input[...] += d_values
     kept.append(l.keep(r.d_input, r.input_grad))
     r.gains[0, 0:1, :] = attn_gain_part
@@ -1202,12 +1224,13 @@
     r.parts[1] = dot(r.active[l.s2], down_all).astype(BF).reshape(8, 32, WIDTH)
     last.cross(r.parts.at[1])
     own_gu_sum.cross()
+    down_b_sum.cross()
     gu_sums[1].step(2)
     qkv_sum.join()
     qkv_sum.step(0)
-    gu_sums[0].step(1)
-    out_sum.start()
-    gu_sums[2].step(2)
+    gu_sums[0].step(2)
+    gu_sums[2].step(1)
+    down_a_sum.step(2)
     r.parts[2] = dot(r.active[l.s1], down_all).astype(BF).reshape(8, 32, WIDTH)
     last.near(r.parts.at[2])
     own = r.middle[...] + dot(r.active[l.s], down_all)
@@ -1215,27 +1238,27 @@
         copy.wait_recv()
     r.gains[1] = r.gains[0] + r.gain_slots[0] + r.gain_slots[1] + r.gain_slots[2]
     gains_y = l.push(r.gains.at[1], r.gain_slots.at[3], dp=l.y_peer)
-    gu_sums[0].step(2)
+    out_sum.join()
+    out_sum.step(0)
+    r.gu_all[l.dp, l.s1] = gu_sums[0].total().astype(BF)
+    home.append(l.push(r.gu_all.at[l.dp, l.s1], r.gu_grad.at[l.s], s=l.s1))
     r.gu_all[l.dp, l.s2] = gu_sums[1].total().astype(BF)
     home.append(l.push(r.gu_all.at[l.dp, l.s2], r.gu_grad.at[l.s], s=l.s2))
+    gu_sums[2].step(2)
     qkv_sum.step(1)
-    out_sum.join()
-    out_sum.step(0)
-    r.gu_all[l.dp, l.s3] = gu_sums[2].total().astype(BF)
-    home.append(l.push(r.gu_all.at[l.dp, l.s3], r.gu_grad.at[l.s], s=l.s3))
     r.down_own[0:SUM_A] = down_a_sum.total()
     kept.append(l.keep(r.down_own.at[pl.ds(0, SUM_A)], r.down_grad.at[pl.ds(0, SUM_A)]))
     qkv_sum.step(2)
-    r.gu_all[l.dp, l.s] = own_gu_sum.total().astype(BF)
-    kept.append(l.keep(r.gu_all.at[l.dp, l.s], r.gu_grad.at[l.s]))
-    r.gu_all[l.dp, l.s1] = gu_sums[0].total().astype(BF)
-    home.append(l.push(r.gu_all.at[l.dp, l.s1], r.gu_grad.at[l.s], s=l.s1))
-    out_sum.step(1)
+    r.gu_all[l.dp, l.s3] = gu_sums[2].total().astype(BF)
+    home.append(l.push(r.gu_all.at[l.dp, l.s3], r.gu_grad.at[l.s], s=l.s3))
     r.output_own[...] = last.total(own).astype(BF)
     kept.append(l.keep(r.output_own, r.output))
     gains_y.wait_recv()
     r.gains[2] = r.gains[1] + r.gain_slots[3]
     gains_z = [l.push(r.gains.at[2], r.gain_slots.at[4 + k], dp=p) for k, p in enumerate(l.z_peers)]
+    out_sum.step(1)
+    r.gu_all[l.dp, l.s] = own_gu_sum.total().astype(BF)
+    kept.append(l.keep(r.gu_all.at[l.dp, l.s], r.gu_grad.at[l.s]))
     r.qkv_all[l.dp] = qkv_sum.total().astype(BF)
     home += [l.push(r.qkv_all.at[l.dp, o], r.qkv_grad.at[l.s], s=o) for o in l.others]
     kept.append(l.keep(r.qkv_all.at[l.dp, l.s], r.qkv_grad.at[l.s]))
@@ -1259,26 +1282,24 @@
 
 
 def lay_out(
-    output, input_grad, down_grad, out_grad, gu_grad, qkv_grad, gains, attn_gain, ffn_gain,
+    output, input_grad, down_grad, out_grad, gu_grad, qkv_grad, gains,
     output_o, input_o, attn_o, query_o, key_o, value_o, q_gain_o, k_gain_o, out_o, ffn_o, gate_o, up_o, down_o,
 ):
     for src, dst in ((output, output_o), (input_grad, input_o), (down_grad, down_o), (out_grad, out_o)):
         dst[...] = src[...]
-    attn_scale = scale = column(as_row(attn_gain))
     for o in range(SEQ):
         for ref, first, size in ((query_o, 0, OWN_Q), (key_o, OWN_Q, OWN_K), (value_o, OWN_Q + OWN_K, OWN_K)):
-            ref[:, o * size : (o + 1) * size] = qkv_grad[o, :, first : first + size].astype(F32) * scale
-    scale = column(as_row(ffn_gain))
+            ref[:, o * size : (o + 1) * size] = qkv_grad[o, :, first : first + size].astype(F32)
     for ref, first in ((gate_o, 0), (up_o, FF_OWN)):
         parts = []
         for j in range(8):
             for o in range(SEQ):
                 part = gu_grad[o, :, first + j * FF_SHARD : first + (j + 1) * FF_SHARD]
-                parts.append(part.astype(F32) * scale)
+                parts.append(part.astype(F32))
         ref[...] = jnp.concatenate(parts, axis=1)
     size = attn_o.shape[0]
-    attn_o[...] = (column(own_lanes(gains[0:1, :], size)) / attn_scale).reshape(size)
-    ffn_o[...] = (column(own_lanes(gains[1:2, :], size)) / scale).reshape(size)
+    attn_o[...] = own_lanes(gains[0:1, :], size).reshape(size)
+    ffn_o[...] = own_lanes(gains[1:2, :], size).reshape(size)
     q_gain_o[...] = (gains[2:3, 0:64] + gains[2:3, 64:128]).reshape(HEAD_SIZE)
     k_gain_o[...] = (gains[2:3, 128:192] + gains[2:3, 192:256]).reshape(HEAD_SIZE)
 
@@ -1292,8 +1313,8 @@
     return jnp.asarray(np.tile(THETA ** (-steps), 4)[None], F32)
 
 
-COLUMN_COPIES = 126
-ROW_COPIES = 45
+COLUMN_COPIES = 133
+ROW_COPIES = 48
 LOCAL_COPIES = 16
 VMEM_BYTES = 63 * 2**20
 
@@ -1351,6 +1372,8 @@
         d_input=((TOK, WIDTH), F32),
         down_own=((FF_SHARD, WIDTH), F32),
         out_own=((32, WIDTH), F32),
+        gain_all=((2 * PLANES, SEQ, 16, 128), BF),
+        gain_rows=((8, WIDTH), F32),
         w_qkv=((SEQ, 32, QKV), BF),
         cosine=((ROW, 128), F32),
         sine=((ROW, 128), F32),
@@ -1438,11 +1461,11 @@
         pl.pallas_call(
             lay_out,
             out_shape=[jax.ShapeDtypeStruct(*shape) for shape in shapes],
-            in_specs=[pl.BlockSpec(memory_space=pltpu.VMEM)] * 9,
+            in_specs=[pl.BlockSpec(memory_space=pltpu.VMEM)] * 7,
             out_specs=[pl.BlockSpec(memory_space=pltpu.VMEM)] * 13,
             compiler_params=pltpu.CompilerParams(vmem_limit_bytes=VMEM_BYTES),
             cost_estimate=pl.CostEstimate(flops=1_000_000, bytes_accessed=10_000_000, transcendentals=0),
-        )(*done, given["attn_gain"], given["ffn_gain"])
+        )(*done)
     )
 
 

time: 200 us -> 203 us (1.015)
  Pallas kernels: 196 us -> 199 us
    pallas_call x1, Pallas kernels: 191 us -> 195 us  [on_device_in_kernels(): pl.pallas_call(body, out_shape=[jax.ShapeDtypeStruct(*result) for result...]
where the time goes in v5:
time: 203 us; the launch traced here: 200 us
  Pallas kernels  199 us (98%)
    pallas_call x1, Pallas kernels, on_device_in_kernels(): pl.pallas_call(body, out_shape=[jax.ShapeDtypeStruct(*result) for result...  195 us
    pallas_call x1, Pallas kernels, on_device_in_kernels(): pl.pallas_call(lay_out, out_shape=[jax.ShapeDtypeStruct(*shape) for shape...  4.06 us

profile of v5, /device:TPU:0, one launch (start us, length us, event | category | flops | bytes accessed | tf_op | source)
XLA Modules:
  0.0 200.1 jit_solution(196255411069154328)
XLA Ops:
  0.7 194.8 %shard_map.246 = (bf16[256,1024]{1,0:T(8,128)(2,1)}, f32[256,1024]{1,0:T(8,128)}, f32[144,1024]{1,0:T(8,128)}, f32[32,1024]{1,0:T(8,128)}, bf16[4,32,2304]{2,1,0...) custom-call(bf16[256,1024]{1,0:T(8,128)(2,1)} %refs_0_.1, bf16[256,1024]{1,0:T(8,128)(2,1)} %refs_1_.1, ...), custom_call_target="tpu_custom_call" | custom-call | flops 30000001024 | bytes 10000000 | tf_op jit(solution)/shard_map/pallas_call | solution.py:1424
  195.5 4.1 %shard_map.247 = (bf16[256,1024]{1,0:T(8,128)(2,1)}, f32[256,1024]{1,0:T(8,128)}, f32[32]{0:T(128)}, f32[32,1024]{1,0:T(8,128)}, f32[32,512]{1,0:T(8,128)}, /*in...) custom-call(bf16[256,1024]{1,0:T(8,128)(2,1)} %get-tuple-element.20., ...), custom_call_target="tpu_custom_call" | custom-call | flops 1000000 | bytes 10000000 | tf_op jit(solution)/shard_map/pallas_call | solution.py:1461
